TPU v7x, 32 devices: a whole 2x2x4 slice. The times are simulated.
32 devices in a mesh: dp: 16 (over z, y, x), fsdp: 2 (over core).
Axes of the slice: x: 2, y: 2, z: 4, core: 2. Of those that a mesh axis runs over, the one named last changes fastest.
Arguments:
- query_global: bfloat16 [2, 64, 56, 56, 256], P(None, ('dp', 'fsdp')), may hold values from -8 to 8
- small_crop_query: bfloat16 [2, 64, 3, 24, 24, 256], P(None, ('dp', 'fsdp')), may hold values from -8 to 8
- small_count: int32 [2, 64], P(None, ('dp', 'fsdp')), may hold values from 0 to 3
- key_global: bfloat16 [2, 64, 56, 56, 256], P(None, ('dp', 'fsdp')), may hold values from -8 to 8
- shuffle_mask: int32 [2, 2], replicated, may hold values from 0 to 31, as said below
- reduce_weight: float32 [256, 128], P('dp', 'fsdp'), may hold values from -0.375 to 0.375
- spatial_weight: float32 [1152, 128], P('dp', 'fsdp'), may hold values from -0.1875 to 0.1875
- expand_weight: float32 [128, 512], P('dp', 'fsdp'), may hold values from -0.5 to 0.5
- shortcut_weight: float32 [256, 512], P('dp', 'fsdp'), may hold values from -0.375 to 0.375
- norm_gains: float32 [1280], replicated, may hold values from 0.5 to 1.5
- norm_shifts: float32 [1280], replicated, may hold values from -0.5 to 0.5
- lagged_reduce: float32 [256, 128], P('dp', 'fsdp'), may hold values from -0.375 to 0.375
- lagged_spatial: float32 [1152, 128], P('dp', 'fsdp'), may hold values from -0.1875 to 0.1875
- lagged_expand: float32 [128, 512], P('dp', 'fsdp'), may hold values from -0.5 to 0.5
- lagged_shortcut: float32 [256, 512], P('dp', 'fsdp'), may hold values from -0.375 to 0.375
- lagged_gains: float32 [1280], replicated, may hold values from 0.5 to 1.5
- lagged_shifts: float32 [1280], replicated, may hold values from -0.5 to 0.5
Outputs:
- loss: float32 [], replicated
- global_grad: bfloat16 [2, 64, 56, 56, 256], P(None, ('dp', 'fsdp'))
- small_grad: bfloat16 [2, 64, 3, 24, 24, 256], P(None, ('dp', 'fsdp'))
- reduce_grad: float32 [256, 128], P('dp', 'fsdp')
- spatial_grad: float32 [1152, 128], P('dp', 'fsdp')
- expand_grad: float32 [128, 512], P('dp', 'fsdp')
- shortcut_grad: float32 [256, 512], P('dp', 'fsdp')
- gains_grad: float32 [1280], replicated
- shifts_grad: float32 [1280], replicated
Inputs may be any that keep to these rules, and one draw needn't show every extreme that they name: The 2 entries of one micro-batch are distinct, and entries come in pairs: shuffle_mask[2 j + 1, s] = shuffle_mask[2 j, s] XOR (31).
All inputs are finite; a program needn't handle non-finite values.
Results may differ from a plain program's by a relative error of at most 0.012.
Values may be sent and summed in bfloat16 or wider, within the bound.
A program may use at most 256 MiB of HBM per device.

v0:
```python
import functools
import types
import jax
import jax.numpy as jnp
from jax import lax
from jax.experimental import pallas as pl
from jax.experimental.pallas import tpu as pltpu
from jax.sharding import PartitionSpec as P

f32, bf16 = jnp.float32, jnp.bfloat16
CIN, CMID, COUT, NORMS = 256, 128, 512, 1280
SIDE, SMALL = 56, 24
BLOCKS = COUT // 128
TEMP, NORM_EPS, UNIT_EPS = 0.2, 1e-05, 1e-06
ROOT_HALF = 0.7071067811865476
DENSITY = 0.3989422804014327


class Field:
    def __init__(self, count, side, row, out_row, ahead):
        self.count, self.side, self.row, self.out_row = count, side, row, out_row
        self.ahead = ahead
        self.half = side // 2
        self.wide = -(-self.half // 16) * 16
        self.area, self.out_area = side * side, (side // 2) ** 2


def field_pair(images, slots):
    big = Field(images, SIDE, 0, 0, 0)
    small = Field(images * slots, SMALL, images * big.area, images * big.out_area, images)
    return big, small


def at(start, size, align=16):
    return pl.ds(pl.multiple_of(start, align), size)


def folded(x):
    return x.reshape(x.shape[0] // 8, 8, x.shape[1]).sum(0)


def dot(a, b):
    return jnp.dot(a, b, preferred_element_type=f32)


def dot_rows(a, b):
    return lax.dot_general(a, b, (((0,), (0,)), ((), ())), preferred_element_type=f32)


def dot_exact(a, b, dims):
    return lax.dot_general(a, b, (dims, ((), ())), precision=lax.Precision.HIGHEST, preferred_element_type=f32)


def gelu_pair(v):
    share = 0.5 + 0.5 * lax.erf(v * ROOT_HALF)
    return v * share, share + v * (DENSITY * jnp.exp(v * v * -0.5))


def gelu_only(v):
    return v * (0.5 + 0.5 * lax.erf(v * ROOT_HALF))


MOMENTUM = 0.999
MESH = pl.DeviceIdType.MESH
PACK = 192
HALF_PACK = PACK // 2
JOB = 48
TURN_ROWS = (48, 16, 32)


def line(vector, start):
    return vector[pl.ds(start, 128)].reshape(1, 128)


def moments(ref, start, size, step, pivot):
    total = jnp.zeros((8, 128), f32)
    square = jnp.zeros((8, 128), f32)
    for k in range(size // step):
        x = ref[at(start + k * step, step, 8)] - pivot
        total += folded(x)
        square += folded(x * x)
    return total, square


def closed(total, square, pivot, count):
    off = total.sum(0, keepdims=True) / count
    spread = jnp.maximum(square.sum(0, keepdims=True) / count - off * off, 0.0)
    return pivot + off, lax.rsqrt(spread + NORM_EPS)


def patches(planes, field, first, crops):
    size = crops * field.half * field.wide
    here = pl.ds(first, crops)
    above = planes[1, here, 0 : field.half].reshape(size, 3 * CMID)
    level = planes[0, here, 0 : field.half].reshape(size, 3 * CMID)
    below = planes[1, here, 1 : field.half + 1].reshape(size, 3 * CMID)
    return jnp.concatenate([above, level, below], axis=1)


def split_planes(hidden, stage, planes, field, crop, row, slot):
    side, wide = field.side, field.wide
    for odd in range(2):
        stage[slot, odd, 8 : 8 + side] = hidden[odd * side : (odd + 1) * side]
    for odd in range(2):
        for tap in range(3):
            column = stage[slot, odd, pl.ds(7 + tap, wide, stride=2)]
            planes[odd, crop, row + odd, :, tap * CMID : (tap + 1) * CMID] = column.astype(bf16)


def even_cells(source, base, field, wide_stage, dense_stage, put):
    side, half = field.side, field.half
    for y in range(half):
        for block in range(CIN // 128):
            slot = y % 4 * 2 + block
            x = source[at(base + y * 2 * side, 2 * side), block * 128 : (block + 1) * 128]
            wide_stage[slot, 0:side] = x.astype(f32)[0:side]
            dense_stage[block, y * half : (y + 1) * half] = wide_stage[slot, pl.ds(0, half, stride=2)]
    for block in range(CIN // 128):
        put(block, dense_stage[block, 0 : field.out_area].astype(bf16))


def flipped(index, mask):
    bit = 1
    while bit <= mask:
        if mask & bit:
            index = index + bit * (1 - 2 * lax.rem(lax.div(index, bit), 2))
        bit *= 2
    return index


def packed_shards(shards, core, store, which):
    first, second, third, fourth = shards
    zero = jnp.zeros
    second = jnp.concatenate([second, zero((second.shape[0], 56), f32)], axis=1)
    second = jnp.concatenate([second, zero((64, 128), f32)], axis=0).T[0:72, 0:64]
    for start, part in ((0, first), (16, second)):
        rows, lanes = part.shape
        left = jnp.concatenate([part, zero((rows, lanes), f32)], axis=1)
        right = jnp.concatenate([zero((rows, lanes), f32), part], axis=1)
        value = jnp.where(core == 0, left, right)
        if rows % 16:
            value = jnp.concatenate([value, zero((16 - rows % 16, 128), f32)], axis=0)
        store[which, start : start + value.shape[0]] = value.astype(bf16)
    for pair in range(2):
        value = jnp.concatenate([third[:, 0:128], third[:, 128:256]], axis=0)
        value = jnp.where(core == pair, value, 0.0)
        store[which, 96 + pair * 16 : 112 + pair * 16] = value.astype(bf16)
        for block in range(2):
            value = jnp.where(core == pair, fourth[:, block * 128 : (block + 1) * 128], 0.0)
            start = 128 + (pair * 2 + block) * 16
            store[which, start : start + 16] = value.astype(bf16)


def unpacked(gathered, which, chips, weights, stage):
    w1, w2, w3, w4 = weights

    def turn(i, _):
        w1[at(i * 16, 16)] = gathered[which, i, 0:16]
        stage[at(i * 72, 72, 8)] = gathered[which, i, 16:96].astype(f32)[0:72]
        for block in range(BLOCKS):
            lanes = slice(block * 128, (block + 1) * 128)
            w4[at(i * 16, 16), lanes] = gathered[which, i, 128 + block * 16 : 144 + block * 16]
        return 0

    lax.fori_loop(0, chips, turn, 0)
    w2[...] = stage[0 : 9 * CMID].astype(bf16)

    def pairs(i, _):
        a = gathered[which, i * 2, 96:128].astype(f32)
        b = gathered[which, i * 2 + 1, 96:128].astype(f32)
        for block in range(BLOCKS):
            rows = slice(block * 8, (block + 1) * 8)
            w3[at(i * 16, 16), block * 128 : (block + 1) * 128] = jnp.concatenate([a[rows], b[rows]], axis=0).astype(bf16)
        return 0

    lax.fori_loop(0, chips // 2, pairs, 0)


def step_kernel(axes, own, slots, names, *refs):
    r = types.SimpleNamespace(**dict(zip(names, refs)))
    chips, cores = axes
    devices = chips * cores
    lows = 1 << (devices.bit_length() // 2)
    highs = devices // lows
    counts, mask = r.counts, r.mask
    micros, images = counts.shape
    fields = field_pair(images, slots)
    big, small = fields
    crops = images * (1 + slots)
    field_rows = small.row + small.count * small.area
    outs = small.out_row + small.count * small.out_area
    chip, core = lax.axis_index("dp"), lax.axis_index("fsdp")
    me = chip * cores + core
    sibling = (chip, 1 - core)
    field, a1, slope1, a2, even, wide, slope3 = (r.field, r.a1, r.slope1, r.a2, r.even, r.wide, r.slope3)
    thin, gy2, vec, sums, keys = (r.thin, r.gy2, r.vec, r.sums, r.keys)
    planes_of = {0: r.planes_big, images: r.planes_small}
    back_of = {0: r.back_big, images: r.back_small}
    stage_of = {0: r.stage_big, images: r.stage_small}
    wide_stage, dense_stage = r.wide_stage, r.dense_stage
    wq = [r.w1q, r.w2q, r.w3q, r.w4q]
    wk = [r.w1k, r.w2k, r.w3k, r.w4k]
    grads = [r.g1, r.g2, r.g3, r.g4]
    gains, shifts, gains1, shifts1 = (r.gains, r.shifts, r.gains1, r.shifts1)
    gain_sum, shift_sum, loss_sum = r.gain_sum, r.shift_sum, r.loss_sum
    A3, AP, H2, SLOPE2 = 0, BLOCKS * outs, 0, outs

    def place(device):
        return (lax.div(device, cores), lax.rem(device, cores))

    def remote(source, target, send, receive, device):
        return pltpu.make_async_remote_copy(
            src_ref=source, dst_ref=target, send_sem=send, recv_sem=receive, device_id=device, device_id_type=MESH)

    def repeat(first, last, body):
        lax.fori_loop(first, last, lambda k, _: (body(k), 0)[1], 0)

    key_base = field_rows
    key_loads = [
        pltpu.make_async_copy(
            r.key_hbm.at[i // 2, pl.ds(i % 2 * big.area, big.area)],
            field.at[pl.ds(key_base + i * big.area, big.area)], r.key_load.at[i])
        for i in range(2 * micros)
    ]

    def query_loads(m):
        return [
            pltpu.make_async_copy(
                r.big_hbm.at[m], field.at[pl.ds(m * field_rows, small.row)], r.query_load.at[m, 0]),
            pltpu.make_async_copy(
                r.small_hbm.at[m], field.at[pl.ds(m * field_rows + small.row, field_rows - small.row)],
                r.query_load.at[m, 1]),
        ]

    def store_big(m, c):
        return pltpu.make_async_copy(
            field.at[pl.ds(m * field_rows + c * big.area, big.area)],
            r.big_out.at[m, pl.ds(c * big.area, big.area)], r.store.at[m, c])

    def store_small(m):
        return pltpu.make_async_copy(
            field.at[pl.ds(m * field_rows + small.row, field_rows - small.row)], r.small_out.at[m],
            r.store.at[m, images])

    own_half = pl.ds(pl.multiple_of(core * HALF_PACK, HALF_PACK), HALF_PACK)

    def core_copy(which):
        return remote(r.sent.at[which], r.swapped_in.at[which], r.core_send.at[which], r.core_recv.at[which], sibling)

    def wide_copy(which, k):
        here = r.gathered.at[which, chip, own_half]
        return remote(here, here, r.wide_send.at[which, k], r.wide_recv.at[which, k], (lax.rem(chip + k, chips), core))

    def join_copy(which):
        here = r.gathered.at[which, :, own_half]
        return remote(here, here, r.join_send.at[which], r.join_recv.at[which], sibling)

    def spread_start(which):
        core_copy(which).wait()
        r.gathered[which, chip, own_half] = r.sent[which, own_half] + r.swapped_in[which, own_half]
        repeat(1, chips, lambda k: wide_copy(which, k).start())

    def spread_join(which):
        repeat(1, chips, lambda k: wide_copy(which, k).wait())
        join_copy(which).start()

    lower, upper = r.lower, r.upper

    def low_copy(turn, k):
        return remote(
            lower[turn].at[0], lower[turn].at[k], r.low_send.at[turn, k], r.low_recv.at[turn, k], place(flipped(me, k)))

    def high_copy(turn, k):
        return remote(
            upper[turn].at[0], upper[turn].at[k], r.high_send.at[turn, k], r.high_recv.at[turn, k],
            place(flipped(me, k * lows)))

    def exchange_start(turn):
        for k in range(1, lows):
            low_copy(turn, k).start()

    def exchange_middle(turn):
        for k in range(1, lows):
            low_copy(turn, k).wait()
        half = TURN_ROWS[turn] // micros
        for m in range(micros):
            pick = lax.rem(jnp.bitwise_xor(mask[m, 0], mask[m, 1]), lows)
            upper[turn][0, m * half : (m + 1) * half] = lower[turn][pick, m * half : (m + 1) * half]
        for k in range(1, highs):
            high_copy(turn, k).start()

    def exchange_end(turn):
        for k in range(1, highs):
            high_copy(turn, k).wait()

    def put_moments(turn, row, start, size, step):
        pivot = folded(wide[at(start, step, 8)]).sum(0, keepdims=True) / step
        total, square = moments(wide, start, size, step, pivot)
        off = total.sum(0, keepdims=True) / size
        lower[turn][0, pl.ds(row, 1)] = pivot + off
        lower[turn][0, pl.ds(row + 1, 1)] = jnp.maximum(square.sum(0, keepdims=True) - off * off * size, 0.0)

    def combined(turn, m, row, other, count):
        pick = lax.div(jnp.bitwise_xor(mask[m, 0], mask[m, 1]), lows)
        mean, spread = lower[turn][0, pl.ds(row, 1)], lower[turn][0, pl.ds(row + 1, 1)]
        mean2, spread2 = upper[turn][pick, pl.ds(other, 1)], upper[turn][pick, pl.ds(other + 1, 1)]
        apart = mean - mean2
        variance = (spread + spread2 + apart * apart * (count * 0.5)) / (2.0 * count)
        return (mean + mean2) * 0.5, lax.rsqrt(variance + NORM_EPS)

    def affine(group, start):
        mean, root = group
        new_gain = MOMENTUM * line(gains1, start) + (1.0 - MOMENTUM) * line(gains, start)
        new_shift = MOMENTUM * line(shifts1, start) + (1.0 - MOMENTUM) * line(shifts, start)
        scale = root * new_gain
        return scale, new_shift - mean * scale

    area, out_area = float(big.area), float(big.out_area)
    first_row = BLOCKS * outs
    spare = 2 * big.area

    def key_even(i):
        def put(block, value):
            slope3[at((i * 2 + block) * big.out_area, big.out_area)] = value

        even_cells(field, key_base + i * big.area, big, wide_stage, dense_stage, put)

    def key_side(i, start):
        cells = [slope3[at((i * 2 + block) * big.out_area, big.out_area)] for block in range(2)]
        value = dot(jnp.concatenate(cells, axis=1), wk[3][...])
        for block in range(BLOCKS):
            wide[at(start + block * big.out_area, big.out_area)] = value[:, block * 128 : (block + 1) * 128]

    def key_third(m, c, start):
        value = dot(thin[at(m * outs + c * big.out_area, big.out_area)], wk[2][...])
        for block in range(BLOCKS):
            wide[at(start + block * big.out_area, big.out_area)] = value[:, block * 128 : (block + 1) * 128]

    def key_a(i):
        m, c = lax.div(i, 2), lax.rem(i, 2)
        start = m * first_row + c * big.area
        wide[at(start, big.area)] = dot(field[at(key_base + i * big.area, big.area)], wk[0][...])
        put_moments(0, m * 24 + c * 2, start, big.area, 112)
        start = m * first_row + spare
        key_side(i, start)
        for block in range(BLOCKS):
            put_moments(0, m * 24 + 8 + (c * BLOCKS + block) * 2, start + block * big.out_area, big.out_area, 112)

    def key_b(i):
        m, c = lax.div(i, 2), lax.rem(i, 2)
        scale, bias = affine(combined(0, m, m * 24 + c * 2, m * 24 + (1 - c) * 2, area), 0)

        def rows_of(y):
            for k in range(4):
                row = y * 4 + k
                v = wide[at(m * first_row + c * big.area + row * 2 * SIDE, 2 * SIDE)] * scale + bias
                split_planes(gelu_only(v), stage_of[0], planes_of[0], big, c, row, k % 2)

        repeat(0, big.half // 4, rows_of)
        value = dot(patches(planes_of[0], big, c, 1), wk[1][...])
        start = m * first_row + spare + c * big.out_area
        for k in range(big.half):
            wide[pl.ds(start + k * big.half, big.half)] = value[k * big.wide : k * big.wide + big.half]
        put_moments(1, m * 8 + c * 2, start, big.out_area, 112)

    def key_c(i):
        m, c = lax.div(i, 2), lax.rem(i, 2)
        scale, bias = affine(combined(1, m, m * 8 + c * 2, m * 8 + (1 - c) * 2, out_area), CMID)
        for k in range(big.out_area // 112):
            v = wide[at(m * first_row + spare + c * big.out_area + k * 112, 112)] * scale + bias
            thin[at(m * outs + c * big.out_area + k * 112, 112)] = gelu_only(v).astype(bf16)
        start = m * first_row
        key_third(m, c, start)
        for block in range(BLOCKS):
            put_moments(2, m * 16 + (c * BLOCKS + block) * 2, start + block * big.out_area, big.out_area, 112)

    def key_d(i):
        m, c = lax.div(i, 2), lax.rem(i, 2)
        start = m * first_row
        key_third(m, c, start)
        key_side(i, start + BLOCKS * big.out_area)
        parts = []
        for block in range(BLOCKS):
            lanes = 2 * CMID + block * 128
            row, other = (c * BLOCKS + block) * 2, ((1 - c) * BLOCKS + block) * 2
            scale3, bias3 = affine(combined(2, m, m * 16 + row, m * 16 + other, out_area), lanes)
            scale4, bias4 = affine(combined(0, m, m * 24 + 8 + row, m * 24 + 8 + other, out_area), lanes + COUT)
            bias = bias3 + bias4
            e = jnp.zeros((8, 128), f32)
            for k in range(big.out_area // 112):
                x3 = wide[at(start + block * big.out_area + k * 112, 112)]
                x4 = wide[at(start + (BLOCKS + block) * big.out_area + k * 112, 112)]
                e += folded(gelu_only(x3 * scale3 + x4 * scale4 + bias))
            parts.append(e.sum(0, keepdims=True) / out_area)
        length = sum(jnp.sum(part * part, axis=1, keepdims=True) for part in parts)
        inverse = lax.rsqrt(length + UNIT_EPS)
        for block in range(BLOCKS):
            r.embed[pl.ds(m * 8 + c * BLOCKS + block, 1)] = parts[block] * inverse

    def key_copy(k):
        mine = keys.at[pl.ds(pl.multiple_of(me * 16, 16), 16)]
        return remote(r.embed, mine, r.key_send.at[k], r.key_recv.at[k], place(lax.rem(me + k, devices)))

    def share_start():
        keys[at(me * 16, 16)] = r.embed[...]
        repeat(1, devices, lambda k: key_copy(k).start())

    def share_end():
        repeat(1, devices, lambda k: key_copy(k).wait())

    def swap_copy(job):
        return remote(
            r.parts.at[job, 1 - core], r.arrived.at[job], r.swap_send.at[job], r.swap_recv.at[job], sibling)

    def row_copy(job, target, source):
        return remote(
            r.sending.at[job, target], r.landed.at[job, source], r.row_send.at[job, target],
            r.row_recv.at[job, source], (target, core))

    def result_copy(job):
        here = r.packed.at[job, core]
        return remote(here, here, r.result_send.at[job], r.result_recv.at[job], sibling)

    def job_send(job):
        swap_copy(job).wait()

        def turn(k):
            target = lax.rem(chip + k, chips)
            r.sending[job, target] = (r.parts[job, core, target] + r.arrived[job, target]).astype(bf16)
            row_copy(job, target, chip).start()

        repeat(1, chips, turn)
        r.sending[job, chip] = (r.parts[job, core, chip] + r.arrived[job, chip]).astype(bf16)

    def job_sum(job):
        def add(k, total):
            source = lax.rem(chip + chips - k, chips)
            row_copy(job, source, source).wait_recv()
            return total + r.landed[job, source].astype(f32)

        r.packed[job, core] = lax.fori_loop(1, chips, add, r.sending[job, chip].astype(f32))
        result_copy(job).start()

    def job_end(job):
        repeat(1, chips, lambda k: row_copy(job, lax.rem(chip + k, chips), chip).wait_send())
        result_copy(job).wait()

    def fill_head():
        parts, third, fourth = r.parts, grads[2], grads[3]

        def turn(i):
            for block in range(BLOCKS):
                lanes = slice(block * 128, (block + 1) * 128)
                parts[0, 0, i, block * 8 : (block + 1) * 8] = third[at(i * 8, 8, 8), lanes]
                half, row = (0, 32) if block == 0 else (1, (block - 1) * 16)
                parts[0, half, i, row : row + 16] = fourth[at(i * 16, 16), lanes]

        repeat(0, chips, turn)
        swap_copy(0).start()

    def fill_spatial():
        parts = r.parts
        for tile in range(9):
            lanes = slice(tile * 128, (tile + 1) * 128)
            gy2[lanes] = grads[1][:, lanes].T

        def turn(i):
            parts[1, 0, i] = gy2[at(i * 72, JOB, 8)]
            parts[1, 1, i, 0:24] = gy2[at(i * 72 + JOB, 24, 8)]
            parts[1, 1, i, 24:JOB] = jnp.zeros((JOB - 24, 128), f32)

        repeat(0, chips, turn)
        swap_copy(1).start()

    def fill_rest():
        parts = r.parts
        for tile in range(2):
            lanes = slice(tile * 128, (tile + 1) * 128)
            gy2[lanes] = grads[0][:, lanes].T
        column = lax.broadcasted_iota(jnp.int32, (1, 128), 1)
        filler = jnp.zeros((5, 128), f32)
        both = [
            [gain_sum[:, k * 128 : (k + 1) * 128] for k in range(10)] + [jnp.where(column == 0, loss_sum[...], 0.0), filler],
            [shift_sum[:, k * 128 : (k + 1) * 128] for k in range(10)] + [jnp.zeros((1, 128), f32), filler],
        ]
        both = [jnp.concatenate(rows, axis=0) for rows in both]

        def turn(i):
            parts[2, 0, i, 0:16] = gy2[at(i * 16, 16)]
            parts[2, 1, i, 0:16] = jnp.zeros((16, 128), f32)
            for half in range(2):
                parts[2, half, i, 16:32] = both[half]
                parts[2, half, i, 32:48] = jnp.zeros((16, 128), f32)

        repeat(0, chips, turn)
        swap_copy(2).start()

    def rest_send():
        swap_copy(2).wait()

        def value_for(target):
            value = r.parts[2, core, target] + r.arrived[2, target]
            fine = value[16:32] - value[16:32].astype(bf16).astype(f32)
            return jnp.concatenate([value[0:32], fine], axis=0).astype(bf16)

        def turn(k):
            target = lax.rem(chip + k, chips)
            r.sending[2, target] = value_for(target)
            row_copy(2, target, chip).start()

        repeat(1, chips, turn)
        r.sending[2, chip] = value_for(chip)

    for load in query_loads(0) + key_loads:
        load.start()
    barrier = pltpu.get_barrier_semaphore()
    repeat(1, devices, lambda k: pl.semaphore_signal(
        barrier, inc=1, device_id=place(lax.rem(me + k, devices)), device_id_type=MESH))
    if own:
        current = [r.r0[...], r.s0[...], r.e0[...], r.p0[...]]
        lagged = [r.r1[...], r.s1[...], r.e1[...], r.p1[...]]
        packed_shards([MOMENTUM * old + (1.0 - MOMENTUM) * new for old, new in zip(lagged, current)], core, r.sent, 0)
        packed_shards(current, core, r.sent, 1)
    else:
        for shard, w in zip((r.r0, r.s0, r.e0, r.p0, r.r1, r.s1, r.e1, r.p1), wq + wk):
            w[...] = shard[...]
    for ref in list(planes_of.values()) + list(back_of.values()) + list(stage_of.values()) + grads + [
        r.raised, gain_sum, shift_sum, loss_sum, gy2, lower[0], lower[1], lower[2]]:
        ref[...] = jnp.zeros_like(ref)
    pl.semaphore_wait(barrier, devices - 1)
    if own:
        for which in range(2):
            core_copy(which).start()
        for which in range(2):
            spread_start(which)

    def micro_step(m):
        opening, closing = m == 0, m == micros - 1
        base = m * field_rows
        w1, w2, w3, w4 = wq
        w1t, w3t, w4t, wt0, wt1 = (r.w1t, r.w3t, r.w4t, r.wt0, r.wt1)
        alive_count = sum(counts[m, i] for i in range(images)).astype(f32)
        count1 = images * big.area + small.area * alive_count
        count2 = images * big.out_area + small.out_area * alive_count

        def living(kind, crop):
            if kind is big:
                return jnp.float32(1.0)
            return jnp.where(lax.rem(crop, slots) < counts[m, lax.div(crop, slots)], 1.0, 0.0)

        def step_of(kind):
            return 112 if kind is big else 144

        def over_big(body):
            repeat(0, big.count, lambda c: body(big, c, 1))

        def over_small(body):
            body(small, 0, small.count)

        def add_moments(ref, offset, kind, first, count, row0, size, row, where, opener):
            start = offset + row0 + first * size
            if kind is big:

                @pl.when(first == 0)
                def _():
                    vec[row : row + 1] = folded(ref[at(start, opener, 8)]).sum(0, keepdims=True) / opener

            for c in range(count):
                total, square = moments(ref, start + c * size, size, step_of(kind), vec[row : row + 1])
                alive = living(kind, first + c)
                sums[where] += total * alive
                sums[where + 1] += square * alive

        for load in query_loads(m):
            load.wait()

        def even_batch(kind, first, count):
            for c in range(count):
                start = kind.out_row + (first + c) * kind.out_area

                def put(block, value):
                    even[at(start, kind.out_area), block * 128 : (block + 1) * 128] = value

                even_cells(field, base + kind.row + (first + c) * kind.area, kind, wide_stage, dense_stage, put)

        over_big(even_batch)
        over_small(even_batch)

        @pl.when(opening)
        def _():
            for load in key_loads:
                load.wait()
            repeat(0, 2 * micros, key_even)
            if own:
                spread_join(0)
                join_copy(0).wait()
                unpacked(r.gathered, 0, chips, wk, gy2)
            repeat(0, 2 * micros, key_a)
            exchange_start(0)
            for load in query_loads(1):
                load.start()
            if own:
                spread_join(1)
                join_copy(1).wait()
                unpacked(r.gathered, 1, chips, wq, gy2)
            w1t[...] = w1[...].T
            w3t[...] = w3[...].T
            w4t[...] = w4[...].T
            wt0[...] = jnp.zeros_like(wt0)
            wt1[...] = jnp.zeros_like(wt1)

            def tap(ky, kx):
                start = (3 * ky + kx) * CMID
                return w2[start : start + CMID, :].T

            wt0[0:128, 0:128] = tap(1, 1)
            wt0[0:128, 128:256] = tap(1, 2)
            wt0[128:256, 128:256] = tap(1, 0)
            wt1[0:128, 0:128] = tap(2, 1)
            wt1[0:128, 128:256] = tap(2, 2)
            wt1[128:256, 128:256] = tap(2, 0)
            wt1[256:384, 0:128] = tap(0, 1)
            wt1[256:384, 128:256] = tap(0, 2)
            wt1[384:512, 128:256] = tap(0, 0)

        sums[...] = jnp.zeros_like(sums)

        def reduce_batch(kind, first, count):
            start = kind.row + first * kind.area
            size = count * kind.area
            a1[at(start, size)] = dot(field[at(base + start, size)], w1[...])
            add_moments(a1, 0, kind, first, count, kind.row, kind.area, 0, 0, 784)

        over_big(reduce_batch)

        @pl.when(opening)
        def _():
            exchange_middle(0)

        over_small(reduce_batch)
        mean1, root1 = closed(sums[0], sums[1], vec[0:1], count1)
        scale1 = root1 * line(gains, 0)
        bias1 = line(shifts, 0) - mean1 * scale1
        vec[1:2], vec[2:3], vec[3:4], vec[4:5] = mean1, root1, scale1, bias1

        @pl.when(opening)
        def _():
            exchange_end(0)
            repeat(0, 2 * micros, key_b)
            exchange_start(1)

        sums[...] = jnp.zeros_like(sums)

        def hidden_batch(kind, first, count):
            scale, bias = vec[3:4], vec[4:5]
            for c in range(count):
                for k in range(kind.half):
                    start = kind.row + (first + c) * kind.area + k * 2 * kind.side
                    v = a1[at(start, 2 * kind.side)] * scale + bias
                    hidden, slope = gelu_pair(v)
                    slope1[at(start, 2 * kind.side)] = slope.astype(bf16)
                    split_planes(hidden, stage_of[kind.ahead], planes_of[kind.ahead], kind, first + c, k, k % 2)

        over_big(hidden_batch)

        @pl.when(opening)
        def _():
            exchange_middle(1)

        over_small(hidden_batch)

        @pl.when(opening)
        def _():
            exchange_end(1)
            repeat(0, 2 * micros, key_c)
            exchange_start(2)

        def spatial_batch(kind, first, count):
            half, lanes = kind.half, kind.wide
            value = dot(patches(planes_of[kind.ahead], kind, first, count), w2[...])
            start = kind.out_row + first * kind.out_area
            for k in range(count * half):
                a2[pl.ds(start + k * half, half)] = value[k * lanes : k * lanes + half]
            add_moments(a2, 0, kind, first, count, kind.out_row, kind.out_area, 0, 16, 784)

        over_big(spatial_batch)

        @pl.when(opening)
        def _():
            exchange_middle(2)

        over_small(spatial_batch)
        mean2, root2 = closed(sums[16], sums[17], vec[0:1], count2)
        scale2 = root2 * line(gains, CMID)
        bias2 = line(shifts, CMID) - mean2 * scale2
        vec[5:6], vec[6:7], vec[7:8], vec[8:9] = mean2, root2, scale2, bias2

        @pl.when(opening)
        def _():
            exchange_end(2)
            repeat(0, 2 * micros, key_d)
            share_start()

        def head_product(which, source, weight, kind, first, count):
            start = kind.out_row + first * kind.out_area
            size = count * kind.out_area
            value = dot(source, weight[...])
            for block in range(BLOCKS):
                offset = (which * BLOCKS + block) * outs
                wide[at(offset + start, size)] = value[:, block * 128 : (block + 1) * 128]
            for block in range(BLOCKS):
                offset = (which * BLOCKS + block) * outs
                add_moments(
                    wide, offset, kind, first, count, kind.out_row, kind.out_area,
                    16 + which * 4 + block, which * 8 + block * 2, 784)

        def expand_batch(kind, first, count):
            start = kind.out_row + first * kind.out_area
            size, step = count * kind.out_area, step_of(kind)
            scale, bias = vec[7:8], vec[8:9]
            head_product(1, even[at(start, size)], w4, kind, first, count)
            for k in range(size // step):
                hidden, slope = gelu_pair(a2[at(start + k * step, step)] * scale + bias)
                thin[at(H2 + start + k * step, step)] = hidden.astype(bf16)
                thin[at(SLOPE2 + start + k * step, step)] = slope.astype(bf16)
            head_product(0, thin[at(H2 + start, size)], w3, kind, first, count)

        over_big(expand_batch)
        over_small(expand_batch)
        for which in range(2):
            for block in range(BLOCKS):
                row = which * 4 + block
                where = which * 8 + block * 2
                lanes = 2 * CMID + row * 128
                mean, root = closed(sums[where], sums[where + 1], vec[16 + row : 17 + row], count2)
                scale = root * line(gains, lanes)
                bias = line(shifts, lanes) - mean * scale
                vec[24 + row : 25 + row], vec[32 + row : 33 + row] = mean, root
                vec[40 + row : 41 + row] = scale
                if which == 0:
                    vec[48 + block : 49 + block] = bias
                else:
                    vec[48 + block : 49 + block] += bias

        rows_e, rows_c = r.rows_e, r.rows_c

        def embed_batch(kind, first, count):
            step = step_of(kind)
            for c in range(count):
                start = kind.out_row + (first + c) * kind.out_area
                for block in range(BLOCKS):
                    mean3, mean4 = vec[24 + block : 25 + block], vec[28 + block : 29 + block]
                    scale3, scale4 = vec[40 + block : 41 + block], vec[44 + block : 45 + block]
                    bias = vec[48 + block : 49 + block]
                    zero = jnp.zeros((8, 128), f32)
                    e, s0, s3, s4 = zero, zero, zero, zero
                    for k in range(kind.out_area // step):
                        inside = block * outs + start + k * step
                        x3, x4 = wide[at(A3 + inside, step)], wide[at(AP + inside, step)]
                        value, slope = gelu_pair(x3 * scale3 + x4 * scale4 + bias)
                        slope3[at(inside, step)] = slope.astype(bf16)
                        e += folded(value)
                        s0 += folded(slope)
                        s3 += folded(slope * (x3 - mean3))
                        s4 += folded(slope * (x4 - mean4))
                    row = kind.ahead + first + c
                    for which, value in enumerate((e / kind.out_area, s0, s3, s4)):
                        rows_e[which, block, pl.ds(row, 1)] = value.sum(0, keepdims=True)

        over_big(embed_batch)
        over_small(embed_batch)

        @pl.when(opening)
        def _():
            share_end()

        def joined(which):
            return jnp.concatenate([rows_e[which, block] for block in range(BLOCKS)], axis=1)

        e = joined(0)
        inverse = lax.rsqrt(jnp.sum(e * e, axis=-1, keepdims=True) + UNIT_EPS)
        row = lax.broadcasted_iota(jnp.int32, (crops, 1), 0)
        owner = jnp.zeros((crops, 1), jnp.int32)
        live = jnp.where(row < images, 1.0, 0.0)
        for i in range(images):
            owner = jnp.where(row == i, i, owner)
            for slot in range(slots):
                here = row == images + i * slots + slot
                owner = jnp.where(here, i, owner)
                live = jnp.where(here, jnp.where(slot < counts[m, i], 1.0, 0.0), live)
        embedding = e * inverse
        key_blocks = [
            jnp.concatenate(
                [keys[pl.ds(m * 8 + c * BLOCKS + block, devices, stride=16)] for c in range(images)], axis=0)
            for block in range(BLOCKS)
        ]
        logits = sum(
            dot_exact(embedding[:, block * 128 : (block + 1) * 128], key_blocks[block], ((1,), (1,)))
            for block in range(BLOCKS)
        )
        logits = logits / TEMP
        top = jnp.max(logits, axis=-1, keepdims=True)
        powers = jnp.exp(logits - top)
        total = jnp.sum(powers, axis=-1, keepdims=True)
        column = lax.broadcasted_iota(jnp.int32, logits.shape, 1)
        mine = column == owner * devices + me
        chosen = jnp.sum(jnp.where(mine, logits, 0.0), axis=-1, keepdims=True)
        ce = (top + jnp.log(total) - chosen) * live
        loss_sum[...] += jnp.sum(ce, axis=0, keepdims=True)
        toward = (powers / total - jnp.where(mine, 1.0, 0.0)) * (live / TEMP)
        back = jnp.concatenate([dot_exact(toward, block, ((1,), (0,))) for block in key_blocks], axis=1)
        de = inverse * back - e * (inverse * inverse * inverse * jnp.sum(e * back, axis=-1, keepdims=True))
        de = de * jnp.where(row < images, 1.0 / big.out_area, 1.0 / small.out_area)
        sum0 = jnp.sum(de * joined(1), axis=0, keepdims=True)
        for which in range(2):
            reach = jnp.sum(de * joined(2 + which), axis=0, keepdims=True)
            for block in range(BLOCKS):
                row = which * 4 + block
                here = slice(block * 128, (block + 1) * 128)
                lanes = slice(2 * CMID + row * 128, 2 * CMID + (row + 1) * 128)
                mean, root, scale = vec[24 + row : 25 + row], vec[32 + row : 33 + row], vec[40 + row : 41 + row]
                along = reach[:, here] * root
                gain_sum[:, lanes] += along
                shift_sum[:, lanes] += sum0[:, here]
                tilt = scale * root * along / count2
                vec[52 + row : 53 + row] = tilt
                vec[60 + row : 61 + row] = scale * sum0[:, here] / count2 - tilt * mean
                rows_c[which, block] = de[:, here] * scale

        sums[...] = jnp.zeros_like(sums)
        d3, dp = r.d3, r.dp

        def head_back(kind, first, count):
            start = kind.out_row + first * kind.out_area
            size, step = count * kind.out_area, step_of(kind)
            for which, store in ((0, d3), (1, dp)):
                for block in range(BLOCKS):
                    lanes = slice(block * 128, (block + 1) * 128)
                    where = which * 4 + block
                    for c in range(count):
                        rise = rows_c[which, block, pl.ds(kind.ahead + first + c, 1)]
                        alive = living(kind, first + c)
                        tilt, level = vec[52 + where : 53 + where] * alive, vec[60 + where : 61 + where] * alive
                        for k in range(kind.out_area // step):
                            inside = c * kind.out_area + k * step
                            here = block * outs + start + inside
                            x = wide[at(which * BLOCKS * outs + here, step)]
                            grad = slope3[at(here, step)].astype(f32) * rise - (x * tilt + level)
                            store[inside : inside + step, lanes] = grad.astype(bf16)
            grad3, gradp = d3[0:size], dp[0:size]
            gy2[at(start, size)] = dot(grad3, w3t[...])
            gradient = dot(gradp, w4t[...])
            for block in range(2):
                wide[at(AP + block * outs + start, size)] = gradient[:, block * 128 : (block + 1) * 128]
            grads[2][...] += dot_rows(thin[at(H2 + start, size)], grad3)
            grads[3][...] += dot_rows(even[at(start, size)], gradp)
            mean = vec[5:6]
            level, reach = jnp.zeros((8, 128), f32), jnp.zeros((8, 128), f32)
            for k in range(size // step):
                here = at(start + k * step, step)
                gy = gy2[here] * thin[at(SLOPE2 + start + k * step, step)].astype(f32)
                gy2[here] = gy
                level += folded(gy)
                reach += folded(gy * (a2[here] - mean))
            sums[0] += level
            sums[1] += reach

        over_big(head_back)
        over_small(head_back)

        if own:

            @pl.when(closing)
            def _():
                fill_head()

        def norm_back(where, lanes, count):
            mean, root, scale = vec[where : where + 1], vec[where + 1 : where + 2], vec[where + 2 : where + 3]
            level = sums[0].sum(0, keepdims=True)
            along = sums[1].sum(0, keepdims=True) * root
            gain_sum[:, lanes] += along
            shift_sum[:, lanes] += level
            tilt = scale * root * along / count
            vec[68:69] = scale
            vec[69:70] = tilt
            vec[70:71] = scale * level / count - tilt * mean

        norm_back(5, slice(CMID, 2 * CMID), count2)
        sums[...] = jnp.zeros_like(sums)

        def spatial_back(kind, first, count):
            half, lanes, side, step = kind.half, kind.wide, kind.side, step_of(kind)
            out_start = kind.out_row + first * kind.out_area
            for c in range(count):
                alive = living(kind, first + c)
                tilt, level = vec[69:70] * alive, vec[70:71] * alive
                for k in range(kind.out_area // step):
                    here = at(out_start + c * kind.out_area + k * step, step)
                    gy2[here] = gy2[here] * vec[68:69] - (a2[here] * tilt + level)
            column = lax.broadcasted_iota(jnp.int32, (lanes, 128), 0)
            store = back_of[kind.ahead]
            for k in range(count * half):
                here = jnp.where(column < half, gy2[pl.ds(out_start + k * half, lanes)], 0.0)
                following = jnp.where(column < half - 1, gy2[pl.ds(out_start + k * half + 1, lanes)], 0.0)
                store[first + k // half, k % half, :, 0:128] = here.astype(bf16)
                store[first + k // half, k % half, :, 128:256] = following.astype(bf16)
            size = count * half * lanes
            near = store[pl.ds(first, count), 0:half].reshape(size, 256)
            beyond = store[pl.ds(first, count), 1 : half + 1].reshape(size, 256)
            upper_rows = dot(near, wt0[...])
            lower_rows = dot(jnp.concatenate([near, beyond], axis=1), wt1[...])
            start = kind.row + first * kind.area
            for k in range(count * half):
                here = slice(k * lanes, k * lanes + half)
                row = start + k * 2 * side
                for odd, value in ((0, upper_rows), (1, lower_rows)):
                    wide[pl.ds(row + odd * side, half, stride=2)] = value[here, 0:128]
                    wide[pl.ds(row + odd * side + 1, half, stride=2)] = value[here, 128:256]
            grads[1][...] += dot_rows(near[:, 0:128], patches(planes_of[kind.ahead], kind, first, count))
            mean = vec[1:2]
            level, reach = jnp.zeros((8, 128), f32), jnp.zeros((8, 128), f32)
            for k in range(count * kind.area // step):
                here = at(start + k * step, step)
                gy = wide[here] * slope1[here].astype(f32)
                wide[here] = gy
                level += folded(gy)
                reach += folded(gy * (a1[here] - mean))
            sums[0] += level
            sums[1] += reach

        over_big(spatial_back)

        if own:

            @pl.when(closing)
            def _():
                job_send(0)

        over_small(spatial_back)
        norm_back(1, slice(0, CMID), count1)

        if own:

            @pl.when(closing)
            def _():
                fill_spatial()

        def reduce_back(kind, first, count):
            step = step_of(kind)
            size = count * kind.area
            start = kind.row + first * kind.area
            rise = vec[68:69]
            for c in range(count):
                alive = living(kind, first + c)
                tilt, level = vec[69:70] * alive, vec[70:71] * alive
                for k in range(kind.area // step):
                    here = at(start + c * kind.area + k * step, step)
                    grad = wide[here] * rise - (a1[here] * tilt + level)
                    slope1[here] = grad.astype(bf16)
            grads[0][...] += dot_rows(slope1[at(start, size)], field[at(base + start, size)])

        over_big(reduce_back)

        if own:

            @pl.when(closing)
            def _():
                job_send(1)

        over_small(reduce_back)

        if own:

            @pl.when(closing)
            def _():
                fill_rest()
                job_sum(0)

        raised = r.raised

        def field_back(kind, first, count):
            half, side = kind.half, kind.side
            size = count * kind.area
            start = kind.row + first * kind.area
            whole = dot(slope1[at(start, size)], w1t[...])
            out_start = kind.out_row + first * kind.out_area
            for k in range(count * half):
                row = k * 2 * side
                for block in range(2):
                    lanes = slice(block * 128, (block + 1) * 128)
                    slot = k % 4 * 2 + block
                    raised[slot, pl.ds(0, half, stride=2)] = wide[pl.ds(AP + block * outs + out_start + k * half, half)]
                    top_row = whole[row : row + side, lanes] + raised[slot, 0:side]
                    both = jnp.concatenate([top_row, whole[row + side : row + 2 * side, lanes]], axis=0)
                    field[at(base + start + row, 2 * side), lanes] = both.astype(bf16)
            if kind is big:
                store_big(m, first).start()
            else:
                store_small(m).start()

        over_big(field_back)

        if own:

            @pl.when(closing)
            def _():
                rest_send()
                job_sum(1)

        over_small(field_back)

    repeat(0, micros, micro_step)
    if own:
        job_sum(2)
        for job in range(3):
            job_end(job)
    for m in range(micros):
        for c in range(images):
            store_big(m, c).wait()
        store_small(m).wait()


def step_pass(axes, own, slots, big, small, key, counts, mask, current, lagged, vectors):
    chips, cores = axes
    devices = chips * cores
    lows = 1 << (devices.bit_length() // 2)
    highs = devices // lows
    micros, images = counts.shape
    one, two = field_pair(images, slots)
    rows = two.row + two.count * two.area
    outs = two.out_row + two.count * two.out_area
    crops = images * (1 + slots)
    vmem = pl.BlockSpec(memory_space=pltpu.VMEM)
    smem = pl.BlockSpec(memory_space=pltpu.SMEM)
    hbm = pl.BlockSpec(memory_space=pl.ANY)
    weights = [(CIN, CMID), (9 * CMID, CMID), (CMID, COUT), (CIN, COUT)]
    totals = dict(
        g1=(CMID, CIN), g2=(CMID, 9 * CMID), g3=(CMID, COUT), g4=(CIN, COUT),
        gain_sum=(1, NORMS), shift_sum=(1, NORMS), loss_sum=(1, 1))
    r0, s0, e0, p0 = ((w, vmem) for w in current)
    r1, s1, e1, p1 = ((w, vmem) for w in lagged)
    gains, shifts, gains1, shifts1 = ((v, vmem) for v in vectors)
    inputs = dict(
        big_hbm=(big, hbm), small_hbm=(small, hbm), key_hbm=(key, hbm), counts=(counts, smem), mask=(mask, smem),
        r0=r0, s0=s0, e0=e0, p0=p0, r1=r1, s1=s1, e1=e1, p1=p1, gains=gains, shifts=shifts, gains1=gains1, shifts1=shifts1)
    outputs = dict(
        big_out=(jax.ShapeDtypeStruct(big.shape, bf16), hbm), small_out=(jax.ShapeDtypeStruct(small.shape, bf16), hbm))
    if own:
        outputs |= dict(packed=(jax.ShapeDtypeStruct((3, 2, JOB, 128), f32), vmem))
    else:
        outputs |= {n: (jax.ShapeDtypeStruct(shape, f32), vmem) for n, shape in totals.items()}

    def buf(dtype, *shape):
        return pltpu.VMEM(shape, dtype)

    def dma(*shape):
        return pltpu.SemaphoreType.DMA(shape)

    scratch = dict(
        field=buf(bf16, rows + 2 * micros * one.area, CIN),
        a1=buf(f32, rows, 128), slope1=buf(bf16, rows, 128),
        planes_big=buf(bf16, 2, one.count, one.half + 1, one.wide, 384),
        planes_small=buf(bf16, 2, two.count, two.half + 1, two.wide, 384),
        a2=buf(f32, outs, 128), thin=buf(bf16, 2 * outs, 128), even=buf(bf16, outs, CIN),
        wide=buf(f32, 2 * BLOCKS * outs, 128), slope3=buf(bf16, BLOCKS * outs, 128),
        back_big=buf(bf16, one.count, one.half + 1, one.wide, 256),
        back_small=buf(bf16, two.count, two.half + 1, two.wide, 256),
        gy2=buf(f32, outs + 16, 128), stage_big=buf(f32, 2, 2, 80, 128), stage_small=buf(f32, 2, 2, 48, 128),
        wide_stage=buf(f32, 8, SIDE, 128), dense_stage=buf(f32, 2, one.out_area, 128), raised=buf(f32, 8, SIDE, 128),
        d3=buf(bf16, two.count * two.out_area, COUT), dp=buf(bf16, two.count * two.out_area, COUT),
        w1t=buf(bf16, CMID, CIN), w3t=buf(bf16, COUT, CMID), w4t=buf(bf16, COUT, CIN),
        wt0=buf(bf16, 256, 256), wt1=buf(bf16, 512, 256), sums=buf(f32, 18, 8, 128), vec=buf(f32, 80, 128),
        rows_e=buf(f32, 4, BLOCKS, crops, 128), rows_c=buf(f32, 2, BLOCKS, crops, 128),
        keys=buf(f32, devices * 16, 128), embed=buf(f32, 16, 128),
        lower=[buf(f32, lows, n, 128) for n in TURN_ROWS], upper=[buf(f32, highs, n, 128) for n in TURN_ROWS],
        key_load=dma(2 * micros), query_load=dma(micros, 2), store=dma(micros, images + 1),
        low_send=dma(3, lows), low_recv=dma(3, lows), high_send=dma(3, highs), high_recv=dma(3, highs),
        key_send=dma(devices), key_recv=dma(devices),
    )
    first, second, third, fourth = (buf(bf16, *shape) for shape in weights)
    scratch |= dict(w1q=first, w2q=second, w3q=third, w4q=fourth, w1k=first, w2k=second, w3k=third, w4k=fourth)
    if own:
        scratch |= {n: buf(f32, *shape) for n, shape in totals.items()}
        scratch |= dict(
            sent=buf(bf16, 2, PACK, 128), swapped_in=buf(bf16, 2, PACK, 128), gathered=buf(bf16, 2, chips, PACK, 128),
            parts=buf(f32, 3, 2, chips, JOB, 128), arrived=buf(f32, 3, chips, JOB, 128),
            sending=buf(bf16, 3, chips, JOB, 128), landed=buf(bf16, 3, chips, JOB, 128),
            core_send=dma(2), core_recv=dma(2), wide_send=dma(2, chips), wide_recv=dma(2, chips),
            join_send=dma(2), join_recv=dma(2), swap_send=dma(3), swap_recv=dma(3),
            row_send=dma(3, chips), row_recv=dma(3, chips), result_send=dma(3), result_recv=dma(3),
        )
    names = list(inputs) + list(outputs) + list(scratch)
    out = pl.pallas_call(
        functools.partial(step_kernel, axes, own, slots, names),
        out_shape=[shape for shape, _ in outputs.values()],
        in_specs=[spec for _, spec in inputs.values()],
        out_specs=[spec for _, spec in outputs.values()],
        scratch_shapes=list(scratch.values()),
        compiler_params=pltpu.CompilerParams(vmem_limit_bytes=63 * 2**20, collective_id=0, has_side_effects=True),
        name="step",
    )(*[array for array, _ in inputs.values()])
    return types.SimpleNamespace(**dict(zip(outputs, out)))


def finish_kernel(device, packed, loss, reduce_out, spatial_out, expand_out, shortcut_out, gains, shifts):
    here = lax.rem(device[0], 2) == 0
    reduce_out[...] = jnp.where(here, packed[2, 0, 0:16, 0:64], packed[2, 0, 0:16, 64:128])
    rows = jnp.concatenate([packed[1, 0], packed[1, 1, 0:24], jnp.zeros((56, 128), f32)], axis=0).T
    spatial_out[...] = jnp.where(here, rows[0:64, 0:72], rows[64:128, 0:72])
    shortcut = [packed[0, 0, 32:48]] + [packed[0, 1, k * 16 : (k + 1) * 16] for k in range(3)]
    for block in range(2):
        lanes = slice(block * 128, (block + 1) * 128)
        first, second = block, block + 2
        expand_out[:, lanes] = jnp.where(
            here, packed[0, 0, first * 8 : first * 8 + 8], packed[0, 0, second * 8 : second * 8 + 8])
        shortcut_out[:, lanes] = jnp.where(here, shortcut[first], shortcut[second])
    for half, ref in enumerate((gains, shifts)):
        for row in range(NORMS // 128):
            ref[pl.ds(row * 128, 128)] = packed[2, half, 16 + row] + packed[2, half, 32 + row]
    loss[...] = packed[2, 0, 26:27, 0:1] + packed[2, 0, 42:43, 0:1]


def finish_pass(device, packed):
    vmem = pl.BlockSpec(memory_space=pltpu.VMEM)
    smem = pl.BlockSpec(memory_space=pltpu.SMEM)
    shapes = [(1, 1), (16, 64), (64, 72), (8, 256), (16, 256), (NORMS,), (NORMS,)]
    return pl.pallas_call(
        finish_kernel,
        out_shape=[jax.ShapeDtypeStruct(shape, f32) for shape in shapes],
        in_specs=[smem, vmem],
        out_specs=[vmem] * 7,
        name="finish",
    )(device, packed)


def gather_weights(shards):
    rows = [lax.all_gather(part, "dp", axis=0, tiled=True) for part in shards]
    return [lax.all_gather(part, "fsdp", axis=1, tiled=True) for part in rows]


def per_device(axes, *args):
    query_global, small_crop_query, small_count, key_global, shuffle_mask = args[:5]
    current, lagged = args[5:9], args[11:15]
    vectors = (args[9], args[10], args[15], args[16])
    micros = query_global.shape[0]
    slots = small_crop_query.shape[2]
    chips, cores = axes
    own = chips == 16 and cores == 2
    if own:
        current = [w.T if i == 1 else w for i, w in enumerate(current)]
        lagged = [w.T if i == 1 else w for i, w in enumerate(lagged)]
    else:
        fresh = [MOMENTUM * old + (1.0 - MOMENTUM) * new for old, new in zip(lagged, current)]
        current = gather_weights([w.astype(bf16) for w in current])
        lagged = gather_weights([w.astype(bf16) for w in fresh])
    out = step_pass(
        axes, own, slots, query_global.reshape(micros, -1, CIN), small_crop_query.reshape(micros, -1, CIN),
        key_global.reshape(micros, -1, CIN), small_count, shuffle_mask, current, lagged, vectors,
    )
    fields = (out.big_out.reshape(query_global.shape), out.small_out.reshape(small_crop_query.shape))
    if own:
        device = (lax.axis_index("dp") * cores + lax.axis_index("fsdp")).astype(jnp.int32).reshape(1)
        loss, first, second, third, fourth, gains_grad, shifts_grad = finish_pass(device, out.packed)
        return (loss.reshape(()), *fields, first, second.T, third, fourth, gains_grad, shifts_grad)
    totals = (out.g1.T, out.g2.T, out.g3, out.g4)
    summed = lax.psum_scatter(totals, "dp", scatter_dimension=0, tiled=True)
    owned = lax.psum_scatter(summed, "fsdp", scatter_dimension=1, tiled=True)
    sums = lax.psum((out.loss_sum, out.gain_sum, out.shift_sum), ("dp", "fsdp"))
    return (sums[0].reshape(()), *fields, *owned, sums[1].reshape(NORMS), sums[2].reshape(NORMS))


def solution(mesh):
    whole, split = P(), P("dp", "fsdp")
    images, crops = P(None, ("dp", "fsdp"), None, None, None), P(None, ("dp", "fsdp"), None, None, None, None)
    axes = (mesh.shape["dp"], mesh.shape["fsdp"])
    return jax.shard_map(
        functools.partial(per_device, axes),
        mesh=mesh,
        in_specs=(images, crops, P(None, ("dp", "fsdp")), images, whole)
        + (split,) * 4 + (whole,) * 2 + (split,) * 4 + (whole,) * 2,
        out_specs=(whole, images, crops) + (split,) * 4 + (whole,) * 2,
        check_vma=False,
    )
```

profile of v0, /device:TPU:0, one launch (start us, length us, event | category | flops | bytes accessed | tf_op | source)
XLA Modules:
  0.0 140.7 jit_solution(10043828968882753399)
XLA Ops:
  0.7 130.5 %step.1 = (bf16[2,6272,256]{2,1,0:T(8,128)(2,1)}, bf16[2,3456,256]{2,1,0:T(8,128)(2,1)}, f32[3,2,48,128]{3,2,1,0:T(8,128)}) custom-call(bf16[2,6272,256]{2,1,0:T(8,128)(2,1)} %bitcast.10, bf16[2,3456,256]{2,1,0:T(8,128)(2,1)} %bitcast.13, bf16[2,6272,256]{2,1,0:T(8,128)(2,1)} %bitcast.11, s32[2,2]{1,0:T(2,128)} %refs_3_.1, s32[2,2]{1,0:T(2,128)} %refs_4_.1, ...), custom_call_target="tpu_custom_call" | custom-call | tf_op jit(solution)/shard_map/step/pallas_call | solution.py:1093
  131.2 1.6 %finish.1 = (f32[1,1]{1,0:T(1,128)}, f32[16,64]{1,0:T(8,128)}, f32[64,72]{1,0:T(8,128)}, f32[8,256]{1,0:T(8,128)}, f32[16,256]{1,0:T(8,128)}, /*index=5*/f32[1280]{0:T(1024)}, f32[1280]{0:T(1024)}) custom-call(s32[1]{0:T(128)} %bitcast.device, f32[3,2,48,128]{3,2,1,0:T(8,128)} %get-tuple-element.19.packed), custom_call_target="tpu_custom_call" | custom-call | tf_op jit(solution)/shard_map/finish/pallas_call | solution.py:1127
  132.8 0.0 copy-start
  132.8 6.1 %copy.28 = bf16[2,2,56,56,256]{4,3,2,1,0:T(8,128)(2,1)} copy(bf16[2,2,56,56,256]{4,3,2,1,0:T(8,128)(2,1)} %bitcast.12) | data formatting | bytes 12845056
  138.9 0.0 copy-done
  138.9 1.8 %copy.29 = bf16[2,2,3,24,24,256]{5,4,3,2,1,0:T(8,128)(2,1)} copy(bf16[2,2,3,24,24,256]{5,4,3,2,1,0:T(8,128)(2,1)S(1)} %bitcast.14) | data formatting | bytes 7077888
Async XLA Ops:
  132.8 6.1 %copy-start = (bf16[2,3456,256]{2,1,0:T(8,128)(2,1)S(1)}, bf16[2,3456,256]{2,1,0:T(8,128)(2,1)}, u32[]{:S(2)}) copy-start(bf16[2,3456,256]{2,1,0:T(8,128)(2,1)} %get-tuple-element.22) | copy-start | bytes 10616836
where the time goes:
time: 141 us
  Pallas kernels  132 us (94%)
  local copies, waits for them, and re-layouts  7.93 us (6%)
    pallas_call x1, Pallas kernels, step_pass(): pl.pallas_call(functools.partial(step_kernel, axes, own, slots, names), o...  130 us
    unnamed x4, local copies, waits for them, and re-layouts  7.93 us

commit v1 on v0

--- a/solution.py
+++ b/solution.py
@@ -62,9 +62,8 @@
 
 MOMENTUM = 0.999
 MESH = pl.DeviceIdType.MESH
-PACK = 192
-HALF_PACK = PACK // 2
-JOB = 48
+PACK = 96
+JOB_ROWS = (48, 48, 32)
 TURN_ROWS = (48, 16, 32)
 
 
@@ -128,60 +127,66 @@
     return index
 
 
-def packed_shards(shards, core, store, which):
+def side_by_side(top, bottom, core):
+    left = lax.broadcasted_iota(jnp.int32, top.shape, 1) < 64
+    if core == 0:
+        return jnp.where(left, top, pltpu.roll(bottom, 64, 1))
+    return jnp.where(left, pltpu.roll(top, 64, 1), bottom)
+
+
+def packed_shards(shards, store, which):
     first, second, third, fourth = shards
     zero = jnp.zeros
     second = jnp.concatenate([second, zero((second.shape[0], 56), f32)], axis=1)
-    second = jnp.concatenate([second, zero((64, 128), f32)], axis=0).T[0:72, 0:64]
-    for start, part in ((0, first), (16, second)):
-        rows, lanes = part.shape
-        left = jnp.concatenate([part, zero((rows, lanes), f32)], axis=1)
-        right = jnp.concatenate([zero((rows, lanes), f32), part], axis=1)
-        value = jnp.where(core == 0, left, right)
-        if rows % 16:
-            value = jnp.concatenate([value, zero((16 - rows % 16, 128), f32)], axis=0)
-        store[which, start : start + value.shape[0]] = value.astype(bf16)
-    for pair in range(2):
-        value = jnp.concatenate([third[:, 0:128], third[:, 128:256]], axis=0)
-        value = jnp.where(core == pair, value, 0.0)
-        store[which, 96 + pair * 16 : 112 + pair * 16] = value.astype(bf16)
-        for block in range(2):
-            value = jnp.where(core == pair, fourth[:, block * 128 : (block + 1) * 128], 0.0)
-            start = 128 + (pair * 2 + block) * 16
-            store[which, start : start + 16] = value.astype(bf16)
+    second = jnp.concatenate([second, zero((64, 128), f32)], axis=0).T[0:80, 0:64]
+    rows = [jnp.concatenate([first[0:8], first[8:16]], axis=1), jnp.concatenate([second[0:40], second[40:80]], axis=1)]
+    rows += [third[:, 0:128], third[:, 128:256], fourth[:, 0:128], fourth[:, 128:256]]
+    store[which] = jnp.concatenate(rows, axis=0).astype(bf16)
 
 
 def unpacked(gathered, which, chips, weights, stage):
     w1, w2, w3, w4 = weights
 
     def turn(i, _):
-        w1[at(i * 16, 16)] = gathered[which, i, 0:16]
-        stage[at(i * 72, 72, 8)] = gathered[which, i, 16:96].astype(f32)[0:72]
+        z, xy = lax.div(i, 4), lax.rem(i, 4)
+        ours = [gathered[which, core, xy, z] for core in range(2)]
+        first, second = (rows[0:48].astype(f32) for rows in ours)
+        left = lax.broadcasted_iota(jnp.int32, (48, 128), 1) < 64
+        top = jnp.where(left, first, pltpu.roll(second, 64, 1))
+        bottom = jnp.where(left, pltpu.roll(first, 64, 1), second)
+        w1[at(i * 16, 16)] = jnp.concatenate([top[0:8], bottom[0:8]], axis=0).astype(bf16)
+        stage[at(i * 72, 40, 8)] = top[8:48]
+        stage[at(i * 72 + 40, 32, 8)] = bottom[8:40]
         for block in range(BLOCKS):
-            lanes = slice(block * 128, (block + 1) * 128)
-            w4[at(i * 16, 16), lanes] = gathered[which, i, 128 + block * 16 : 144 + block * 16]
+            start = 64 + block % 2 * 16
+            w4[at(i * 16, 16), block * 128 : (block + 1) * 128] = ours[block // 2][start : start + 16]
         return 0
 
     lax.fori_loop(0, chips, turn, 0)
     w2[...] = stage[0 : 9 * CMID].astype(bf16)
 
     def pairs(i, _):
-        a = gathered[which, i * 2, 96:128].astype(f32)
-        b = gathered[which, i * 2 + 1, 96:128].astype(f32)
+        z, xy = lax.div(i, 2), lax.rem(i, 2) * 2
         for block in range(BLOCKS):
-            rows = slice(block * 8, (block + 1) * 8)
-            w3[at(i * 16, 16), block * 128 : (block + 1) * 128] = jnp.concatenate([a[rows], b[rows]], axis=0).astype(bf16)
+            rows = slice(block % 2 * 8, block % 2 * 8 + 8)
+            both = [gathered[which, block // 2, xy + k, z, 48:64].astype(f32)[rows] for k in range(2)]
+            w3[at(i * 16, 16), block * 128 : (block + 1) * 128] = jnp.concatenate(both, axis=0).astype(bf16)
         return 0
 
     lax.fori_loop(0, chips // 2, pairs, 0)
+
+
+def stage_widths(devices):
+    bits = devices.bit_length() - 1
+    return (bits + 2) // 3, (bits + 1) // 3, bits // 3
 
 
 def step_kernel(axes, own, slots, names, *refs):
     r = types.SimpleNamespace(**dict(zip(names, refs)))
     chips, cores = axes
     devices = chips * cores
-    lows = 1 << (devices.bit_length() // 2)
-    highs = devices // lows
+    widths = stage_widths(devices)
+    shifts_of = (0, widths[0], widths[0] + widths[1])
     counts, mask = r.counts, r.mask
     micros, images = counts.shape
     fields = field_pair(images, slots)
@@ -191,7 +196,7 @@
     outs = small.out_row + small.count * small.out_area
     chip, core = lax.axis_index("dp"), lax.axis_index("fsdp")
     me = chip * cores + core
-    sibling = (chip, 1 - core)
+    xy, z = lax.rem(chip, 4), lax.div(chip, 4)
     field, a1, slope1, a2, even, wide, slope3 = (r.field, r.a1, r.slope1, r.a2, r.even, r.wide, r.slope3)
     thin, gy2, vec, sums, keys = (r.thin, r.gy2, r.vec, r.sums, r.keys)
     planes_of = {0: r.planes_big, images: r.planes_small}
@@ -242,68 +247,75 @@
             field.at[pl.ds(m * field_rows + small.row, field_rows - small.row)], r.small_out.at[m],
             r.store.at[m, images])
 
-    own_half = pl.ds(pl.multiple_of(core * HALF_PACK, HALF_PACK), HALF_PACK)
-
-    def core_copy(which):
-        return remote(r.sent.at[which], r.swapped_in.at[which], r.core_send.at[which], r.core_recv.at[which], sibling)
-
-    def wide_copy(which, k):
-        here = r.gathered.at[which, chip, own_half]
-        return remote(here, here, r.wide_send.at[which, k], r.wide_recv.at[which, k], (lax.rem(chip + k, chips), core))
-
-    def join_copy(which):
-        here = r.gathered.at[which, :, own_half]
-        return remote(here, here, r.join_send.at[which], r.join_recv.at[which], sibling)
-
-    def spread_start(which):
-        core_copy(which).wait()
-        r.gathered[which, chip, own_half] = r.sent[which, own_half] + r.swapped_in[which, own_half]
-        repeat(1, chips, lambda k: wide_copy(which, k).start())
-
-    def spread_join(which):
-        repeat(1, chips, lambda k: wide_copy(which, k).wait())
-        join_copy(which).start()
-
-    lower, upper = r.lower, r.upper
-
-    def low_copy(turn, k):
-        return remote(
-            lower[turn].at[0], lower[turn].at[k], r.low_send.at[turn, k], r.low_recv.at[turn, k], place(flipped(me, k)))
-
-    def high_copy(turn, k):
-        return remote(
-            upper[turn].at[0], upper[turn].at[k], r.high_send.at[turn, k], r.high_recv.at[turn, k],
-            place(flipped(me, k * lows)))
+    def partner(flip):
+        return place(flipped(me, flip))
+
+    def gather_copies(which, stage):
+        if stage == 0:
+            here = r.gathered.at[which, core, xy, z]
+            flips = [8 * k for k in range(1, chips // 4)]
+        elif stage == 1:
+            here = r.gathered.at[which, core, xy]
+            flips = [2 * k for k in range(1, 4)]
+        else:
+            here = r.gathered.at[which, core]
+            flips = [1]
+        return [
+            remote(here, here, r.gather_send.at[which, stage, k], r.gather_recv.at[which, stage, k], partner(flip))
+            for k, flip in enumerate(flips)
+        ]
+
+    def gather_start(which, stage):
+        for copy in gather_copies(which, stage):
+            copy.start()
+
+    def gather_end(which, stage):
+        for copy in gather_copies(which, stage):
+            copy.wait()
+
+    moved = r.moved
+
+    def exchange_copies(turn, stage):
+        ref = moved[turn][stage]
+        return [
+            remote(
+                ref.at[0], ref.at[k], r.move_send.at[turn, stage, k], r.move_recv.at[turn, stage, k],
+                partner(k << shifts_of[stage]))
+            for k in range(1, 1 << widths[stage])
+        ]
+
+    def picked(m, stage):
+        return lax.rem(lax.div(jnp.bitwise_xor(mask[m, 0], mask[m, 1]), 1 << shifts_of[stage]), 1 << widths[stage])
 
     def exchange_start(turn):
-        for k in range(1, lows):
-            low_copy(turn, k).start()
-
-    def exchange_middle(turn):
-        for k in range(1, lows):
-            low_copy(turn, k).wait()
+        for copy in exchange_copies(turn, 0):
+            copy.start()
+
+    def exchange_next(turn, stage):
+        for copy in exchange_copies(turn, stage - 1):
+            copy.wait()
         half = TURN_ROWS[turn] // micros
         for m in range(micros):
-            pick = lax.rem(jnp.bitwise_xor(mask[m, 0], mask[m, 1]), lows)
-            upper[turn][0, m * half : (m + 1) * half] = lower[turn][pick, m * half : (m + 1) * half]
-        for k in range(1, highs):
-            high_copy(turn, k).start()
+            rows = slice(m * half, (m + 1) * half)
+            moved[turn][stage][0, rows] = moved[turn][stage - 1][picked(m, stage - 1), rows]
+        for copy in exchange_copies(turn, stage):
+            copy.start()
 
     def exchange_end(turn):
-        for k in range(1, highs):
-            high_copy(turn, k).wait()
+        for copy in exchange_copies(turn, 2):
+            copy.wait()
 
     def put_moments(turn, row, start, size, step):
         pivot = folded(wide[at(start, step, 8)]).sum(0, keepdims=True) / step
         total, square = moments(wide, start, size, step, pivot)
         off = total.sum(0, keepdims=True) / size
-        lower[turn][0, pl.ds(row, 1)] = pivot + off
-        lower[turn][0, pl.ds(row + 1, 1)] = jnp.maximum(square.sum(0, keepdims=True) - off * off * size, 0.0)
+        moved[turn][0][0, pl.ds(row, 1)] = pivot + off
+        moved[turn][0][0, pl.ds(row + 1, 1)] = jnp.maximum(square.sum(0, keepdims=True) - off * off * size, 0.0)
 
     def combined(turn, m, row, other, count):
-        pick = lax.div(jnp.bitwise_xor(mask[m, 0], mask[m, 1]), lows)
-        mean, spread = lower[turn][0, pl.ds(row, 1)], lower[turn][0, pl.ds(row + 1, 1)]
-        mean2, spread2 = upper[turn][pick, pl.ds(other, 1)], upper[turn][pick, pl.ds(other + 1, 1)]
+        pick = picked(m, 2)
+        mean, spread = moved[turn][0][0, pl.ds(row, 1)], moved[turn][0][0, pl.ds(row + 1, 1)]
+        mean2, spread2 = moved[turn][2][pick, pl.ds(other, 1)], moved[turn][2][pick, pl.ds(other + 1, 1)]
         apart = mean - mean2
         variance = (spread + spread2 + apart * apart * (count * 0.5)) / (2.0 * count)
         return (mean + mean2) * 0.5, lax.rsqrt(variance + NORM_EPS)
@@ -397,142 +409,158 @@
         for block in range(BLOCKS):
             r.embed[pl.ds(m * 8 + c * BLOCKS + block, 1)] = parts[block] * inverse
 
-    def key_copy(k):
-        mine = keys.at[pl.ds(pl.multiple_of(me * 16, 16), 16)]
-        return remote(r.embed, mine, r.key_send.at[k], r.key_recv.at[k], place(lax.rem(me + k, devices)))
-
-    def share_start():
-        keys[at(me * 16, 16)] = r.embed[...]
-        repeat(1, devices, lambda k: key_copy(k).start())
-
-    def share_end():
-        repeat(1, devices, lambda k: key_copy(k).wait())
-
-    def swap_copy(job):
+    def share_copies(stage):
+        size = 16 << shifts_of[stage]
+        here = keys.at[pl.ds(pl.multiple_of(lax.div(me, 1 << shifts_of[stage]) * size, 16), size)]
+        return [
+            remote(here, here, r.key_send.at[stage, k], r.key_recv.at[stage, k], partner(k << shifts_of[stage]))
+            for k in range(1, 1 << widths[stage])
+        ]
+
+    def share_start(stage):
+        if stage == 0:
+            keys[at(me * 16, 16)] = r.embed[...]
+        for copy in share_copies(stage):
+            copy.start()
+
+    def share_end(stage):
+        for copy in share_copies(stage):
+            copy.wait()
+
+    def core_copy(job):
         return remote(
-            r.parts.at[job, 1 - core], r.arrived.at[job], r.swap_send.at[job], r.swap_recv.at[job], sibling)
-
-    def row_copy(job, target, source):
-        return remote(
-            r.sending.at[job, target], r.landed.at[job, source], r.row_send.at[job, target],
-            r.row_recv.at[job, source], (target, core))
-
-    def result_copy(job):
-        here = r.packed.at[job, core]
-        return remote(here, here, r.result_send.at[job], r.result_recv.at[job], sibling)
-
-    def job_send(job):
-        swap_copy(job).wait()
-
-        def turn(k):
-            target = lax.rem(chip + k, chips)
-            r.sending[job, target] = (r.parts[job, core, target] + r.arrived[job, target]).astype(bf16)
-            row_copy(job, target, chip).start()
-
-        repeat(1, chips, turn)
-        r.sending[job, chip] = (r.parts[job, core, chip] + r.arrived[job, chip]).astype(bf16)
-
-    def job_sum(job):
-        def add(k, total):
-            source = lax.rem(chip + chips - k, chips)
-            row_copy(job, source, source).wait_recv()
-            return total + r.landed[job, source].astype(f32)
-
-        r.packed[job, core] = lax.fori_loop(1, chips, add, r.sending[job, chip].astype(f32))
-        result_copy(job).start()
+            r.parts[job].at[1 - core], r.arrived[job], r.sum_send.at[job, 0, 0], r.sum_recv.at[job, 0, 0], partner(1))
+
+    def plane_copies(job):
+        return [
+            remote(
+                r.plane_out[job].at[k], r.plane_in[job].at[k], r.sum_send.at[job, 1, k], r.sum_recv.at[job, 1, k],
+                partner(2 * k))
+            for k in range(1, 4)
+        ]
+
+    def column_copies(job):
+        return [
+            remote(
+                r.column_out[job].at[k], r.column_in[job].at[k], r.sum_send.at[job, 2, k], r.sum_recv.at[job, 2, k],
+                partner(8 * k))
+            for k in range(1, 4)
+        ]
+
+    def job_plane(job):
+        core_copy(job).wait()
+        own_part, wire = r.parts[job], r.plane_out[job].dtype
+        for k in range(1, 4):
+            far = flipped(xy, k)
+            r.plane_out[job][k] = (own_part[core, far] + r.arrived[job][far]).astype(wire)
+        for copy in plane_copies(job):
+            copy.start()
+        r.arrived[job][xy] = own_part[core, xy] + r.arrived[job][xy]
+
+    def job_column(job):
+        for copy in plane_copies(job):
+            copy.wait()
+        held, wire = r.arrived[job], r.column_out[job].dtype
+        for far in range(4):
+            held[xy, far] += sum(r.plane_in[job][k, far].astype(f32) for k in range(1, 4))
+        for k in range(1, 4):
+            r.column_out[job][k] = held[xy, flipped(z, k)].astype(wire)
+        for copy in column_copies(job):
+            copy.start()
 
     def job_end(job):
-        repeat(1, chips, lambda k: row_copy(job, lax.rem(chip + k, chips), chip).wait_send())
-        result_copy(job).wait()
+        for copy in column_copies(job):
+            copy.wait()
+        start = sum(JOB_ROWS[:job])
+        total = r.arrived[job][xy, z] + sum(r.column_in[job][k].astype(f32) for k in range(1, 4))
+        r.packed[start : start + JOB_ROWS[job]] = total
+
+    def each_chip(body):
+        def turn(i):
+            body(i, lax.rem(i, 4), lax.div(i, 4))
+
+        repeat(0, chips, turn)
 
     def fill_head():
-        parts, third, fourth = r.parts, grads[2], grads[3]
-
-        def turn(i):
+        part, third, fourth = r.parts[0], grads[2], grads[3]
+
+        def turn(i, to_xy, to_z):
             for block in range(BLOCKS):
+                half, row = block // 2, block % 2
                 lanes = slice(block * 128, (block + 1) * 128)
-                parts[0, 0, i, block * 8 : (block + 1) * 8] = third[at(i * 8, 8, 8), lanes]
-                half, row = (0, 32) if block == 0 else (1, (block - 1) * 16)
-                parts[0, half, i, row : row + 16] = fourth[at(i * 16, 16), lanes]
-
-        repeat(0, chips, turn)
-        swap_copy(0).start()
+                part[half, to_xy, to_z, row * 8 : row * 8 + 8] = third[at(i * 8, 8, 8), lanes]
+                part[half, to_xy, to_z, 16 + row * 16 : 32 + row * 16] = fourth[at(i * 16, 16), lanes]
+
+        each_chip(turn)
+        core_copy(0).start()
 
     def fill_spatial():
-        parts = r.parts
+        part = r.parts[1]
         for tile in range(9):
             lanes = slice(tile * 128, (tile + 1) * 128)
             gy2[lanes] = grads[1][:, lanes].T
-
-        def turn(i):
-            parts[1, 0, i] = gy2[at(i * 72, JOB, 8)]
-            parts[1, 1, i, 0:24] = gy2[at(i * 72 + JOB, 24, 8)]
-            parts[1, 1, i, 24:JOB] = jnp.zeros((JOB - 24, 128), f32)
-
-        repeat(0, chips, turn)
-        swap_copy(1).start()
+        filler = jnp.zeros((8, 128), f32)
+
+        def turn(i, to_xy, to_z):
+            top = gy2[at(i * 72, 40, 8)]
+            bottom = jnp.concatenate([gy2[at(i * 72 + 40, 32, 8)], filler], axis=0)
+            for half in range(2):
+                part[half, to_xy, to_z, 0:40] = side_by_side(top, bottom, half)
+                part[half, to_xy, to_z, 40:48] = filler
+
+        each_chip(turn)
+        core_copy(1).start()
 
     def fill_rest():
-        parts = r.parts
+        part = r.parts[2]
         for tile in range(2):
             lanes = slice(tile * 128, (tile + 1) * 128)
             gy2[lanes] = grads[0][:, lanes].T
         column = lax.broadcasted_iota(jnp.int32, (1, 128), 1)
-        filler = jnp.zeros((5, 128), f32)
-        both = [
-            [gain_sum[:, k * 128 : (k + 1) * 128] for k in range(10)] + [jnp.where(column == 0, loss_sum[...], 0.0), filler],
-            [shift_sum[:, k * 128 : (k + 1) * 128] for k in range(10)] + [jnp.zeros((1, 128), f32), filler],
-        ]
-        both = [jnp.concatenate(rows, axis=0) for rows in both]
-
-        def turn(i):
-            parts[2, 0, i, 0:16] = gy2[at(i * 16, 16)]
-            parts[2, 1, i, 0:16] = jnp.zeros((16, 128), f32)
+        filler = jnp.zeros((1, 128), f32)
+        rows = [gain_sum[:, k * 128 : (k + 1) * 128] for k in range(10)]
+        rows += [jnp.where(column == 0, loss_sum[...], 0.0), filler]
+        rows += [shift_sum[:, k * 128 : (k + 1) * 128] for k in range(10)] + [filler, filler]
+        rows = jnp.concatenate(rows, axis=0)
+
+        def turn(i, to_xy, to_z):
             for half in range(2):
-                parts[2, half, i, 16:32] = both[half]
-                parts[2, half, i, 32:48] = jnp.zeros((16, 128), f32)
-
-        repeat(0, chips, turn)
-        swap_copy(2).start()
-
-    def rest_send():
-        swap_copy(2).wait()
-
-        def value_for(target):
-            value = r.parts[2, core, target] + r.arrived[2, target]
-            fine = value[16:32] - value[16:32].astype(bf16).astype(f32)
-            return jnp.concatenate([value[0:32], fine], axis=0).astype(bf16)
-
-        def turn(k):
-            target = lax.rem(chip + k, chips)
-            r.sending[2, target] = value_for(target)
-            row_copy(2, target, chip).start()
-
-        repeat(1, chips, turn)
-        r.sending[2, chip] = value_for(chip)
+                value = side_by_side(gy2[at(i * 16, 8, 8)], gy2[at(i * 16 + 8, 8, 8)], half)
+                part[half, to_xy, to_z] = jnp.concatenate([value, rows], axis=0)
+
+        each_chip(turn)
+        core_copy(2).start()
 
     for load in query_loads(0) + key_loads:
         load.start()
+    flips = {k << shift for width, shift in zip(widths, shifts_of) for k in range(1, 1 << width)}
+    if own:
+        flips |= {1} | {2 * k for k in range(1, 4)} | {8 * k for k in range(1, 4)}
     barrier = pltpu.get_barrier_semaphore()
-    repeat(1, devices, lambda k: pl.semaphore_signal(
-        barrier, inc=1, device_id=place(lax.rem(me + k, devices)), device_id_type=MESH))
+    for flip in sorted(flips):
+        pl.semaphore_signal(barrier, inc=1, device_id=partner(flip), device_id_type=MESH)
     if own:
         current = [r.r0[...], r.s0[...], r.e0[...], r.p0[...]]
         lagged = [r.r1[...], r.s1[...], r.e1[...], r.p1[...]]
-        packed_shards([MOMENTUM * old + (1.0 - MOMENTUM) * new for old, new in zip(lagged, current)], core, r.sent, 0)
-        packed_shards(current, core, r.sent, 1)
+        packed_shards([MOMENTUM * old + (1.0 - MOMENTUM) * new for old, new in zip(lagged, current)], r.sent, 0)
+        packed_shards(current, r.sent, 1)
+        for which in range(2):
+            r.gathered[which, core, xy, z] = r.sent[which]
     else:
         for shard, w in zip((r.r0, r.s0, r.e0, r.p0, r.r1, r.s1, r.e1, r.p1), wq + wk):
             w[...] = shard[...]
-    for ref in list(planes_of.values()) + list(back_of.values()) + list(stage_of.values()) + grads + [
-        r.raised, gain_sum, shift_sum, loss_sum, gy2, lower[0], lower[1], lower[2]]:
-        ref[...] = jnp.zeros_like(ref)
-    pl.semaphore_wait(barrier, devices - 1)
+    if flips:
+        pl.semaphore_wait(barrier, len(flips))
     if own:
         for which in range(2):
-            core_copy(which).start()
+            gather_start(which, 0)
+    for ref in list(planes_of.values()) + list(back_of.values()) + list(stage_of.values()) + grads + [
+        r.raised, gain_sum, shift_sum, loss_sum, gy2, moved[0][0], moved[1][0], moved[2][0]]:
+        ref[...] = jnp.zeros_like(ref)
+    if own:
         for which in range(2):
-            spread_start(which)
+            gather_end(which, 0)
+            gather_start(which, 1)
 
     def micro_step(m):
         opening, closing = m == 0, m == micros - 1
@@ -551,8 +579,16 @@
         def step_of(kind):
             return 112 if kind is big else 144
 
-        def over_big(body):
-            repeat(0, big.count, lambda c: body(big, c, 1))
+        def over_big(body, *hooks):
+            def turn(c):
+                body(big, c, 1)
+                for k, (when, hook) in enumerate(hooks):
+
+                    @pl.when(jnp.logical_and(when, c == k))
+                    def _():
+                        hook()
+
+            repeat(0, big.count, turn)
 
         def over_small(body):
             body(small, 0, small.count)
@@ -592,16 +628,18 @@
                 load.wait()
             repeat(0, 2 * micros, key_even)
             if own:
-                spread_join(0)
-                join_copy(0).wait()
+                gather_end(0, 1)
+                gather_start(0, 2)
+                gather_end(1, 1)
+                gather_start(1, 2)
+                gather_end(0, 2)
                 unpacked(r.gathered, 0, chips, wk, gy2)
             repeat(0, 2 * micros, key_a)
             exchange_start(0)
             for load in query_loads(1):
                 load.start()
             if own:
-                spread_join(1)
-                join_copy(1).wait()
+                gather_end(1, 2)
                 unpacked(r.gathered, 1, chips, wq, gy2)
             w1t[...] = w1[...].T
             w3t[...] = w3[...].T
@@ -631,12 +669,7 @@
             a1[at(start, size)] = dot(field[at(base + start, size)], w1[...])
             add_moments(a1, 0, kind, first, count, kind.row, kind.area, 0, 0, 784)
 
-        over_big(reduce_batch)
-
-        @pl.when(opening)
-        def _():
-            exchange_middle(0)
-
+        over_big(reduce_batch, (opening, lambda: exchange_next(0, 1)), (opening, lambda: exchange_next(0, 2)))
         over_small(reduce_batch)
         mean1, root1 = closed(sums[0], sums[1], vec[0:1], count1)
         scale1 = root1 * line(gains, 0)
@@ -661,12 +694,7 @@
                     slope1[at(start, 2 * kind.side)] = slope.astype(bf16)
                     split_planes(hidden, stage_of[kind.ahead], planes_of[kind.ahead], kind, first + c, k, k % 2)
 
-        over_big(hidden_batch)
-
-        @pl.when(opening)
-        def _():
-            exchange_middle(1)
-
+        over_big(hidden_batch, (opening, lambda: exchange_next(1, 1)), (opening, lambda: exchange_next(1, 2)))
         over_small(hidden_batch)
 
         @pl.when(opening)
@@ -683,12 +711,7 @@
                 a2[pl.ds(start + k * half, half)] = value[k * lanes : k * lanes + half]
             add_moments(a2, 0, kind, first, count, kind.out_row, kind.out_area, 0, 16, 784)
 
-        over_big(spatial_batch)
-
-        @pl.when(opening)
-        def _():
-            exchange_middle(2)
-
+        over_big(spatial_batch, (opening, lambda: exchange_next(2, 1)), (opening, lambda: exchange_next(2, 2)))
         over_small(spatial_batch)
         mean2, root2 = closed(sums[16], sums[17], vec[0:1], count2)
         scale2 = root2 * line(gains, CMID)
@@ -699,7 +722,7 @@
         def _():
             exchange_end(2)
             repeat(0, 2 * micros, key_d)
-            share_start()
+            share_start(0)
 
         def head_product(which, source, weight, kind, first, count):
             start = kind.out_row + first * kind.out_area
@@ -725,8 +748,17 @@
                 thin[at(SLOPE2 + start + k * step, step)] = slope.astype(bf16)
             head_product(0, thin[at(H2 + start, size)], w3, kind, first, count)
 
-        over_big(expand_batch)
+        def share_next(stage):
+            share_end(stage - 1)
+            share_start(stage)
+
+        over_big(expand_batch, (opening, lambda: None), (opening, lambda: share_next(1)))
         over_small(expand_batch)
+
+        @pl.when(opening)
+        def _():
+            share_next(2)
+
         for which in range(2):
             for block in range(BLOCKS):
                 row = which * 4 + block
@@ -772,7 +804,7 @@
 
         @pl.when(opening)
         def _():
-            share_end()
+            share_end(2)
 
         def joined(which):
             return jnp.concatenate([rows_e[which, block] for block in range(BLOCKS)], axis=1)
@@ -928,14 +960,10 @@
             sums[0] += level
             sums[1] += reach
 
-        over_big(spatial_back)
-
-        if own:
-
-            @pl.when(closing)
-            def _():
-                job_send(0)
-
+        def job_hooks(job):
+            return ((closing, lambda: job_plane(job)), (closing, lambda: job_column(job))) if own else ()
+
+        over_big(spatial_back, *job_hooks(0))
         over_small(spatial_back)
         norm_back(1, slice(0, CMID), count1)
 
@@ -944,6 +972,7 @@
             @pl.when(closing)
             def _():
                 fill_spatial()
+                job_end(0)
 
         def reduce_back(kind, first, count):
             step = step_of(kind)
@@ -959,14 +988,7 @@
                     slope1[here] = grad.astype(bf16)
             grads[0][...] += dot_rows(slope1[at(start, size)], field[at(base + start, size)])
 
-        over_big(reduce_back)
-
-        if own:
-
-            @pl.when(closing)
-            def _():
-                job_send(1)
-
+        over_big(reduce_back, *job_hooks(1))
         over_small(reduce_back)
 
         if own:
@@ -974,7 +996,7 @@
             @pl.when(closing)
             def _():
                 fill_rest()
-                job_sum(0)
+                job_end(1)
 
         raised = r.raised
 
@@ -998,22 +1020,12 @@
             else:
                 store_small(m).start()
 
-        over_big(field_back)
-
-        if own:
-
-            @pl.when(closing)
-            def _():
-                rest_send()
-                job_sum(1)
-
+        over_big(field_back, *job_hooks(2))
         over_small(field_back)
 
     repeat(0, micros, micro_step)
     if own:
-        job_sum(2)
-        for job in range(3):
-            job_end(job)
+        job_end(2)
     for m in range(micros):
         for c in range(images):
             store_big(m, c).wait()
@@ -1023,8 +1035,7 @@
 def step_pass(axes, own, slots, big, small, key, counts, mask, current, lagged, vectors):
     chips, cores = axes
     devices = chips * cores
-    lows = 1 << (devices.bit_length() // 2)
-    highs = devices // lows
+    widths = stage_widths(devices)
     micros, images = counts.shape
     one, two = field_pair(images, slots)
     rows = two.row + two.count * two.area
@@ -1046,7 +1057,7 @@
     outputs = dict(
         big_out=(jax.ShapeDtypeStruct(big.shape, bf16), hbm), small_out=(jax.ShapeDtypeStruct(small.shape, bf16), hbm))
     if own:
-        outputs |= dict(packed=(jax.ShapeDtypeStruct((3, 2, JOB, 128), f32), vmem))
+        outputs |= dict(packed=(jax.ShapeDtypeStruct((sum(JOB_ROWS), 128), f32), vmem))
     else:
         outputs |= {n: (jax.ShapeDtypeStruct(shape, f32), vmem) for n, shape in totals.items()}
 
@@ -1072,22 +1083,24 @@
         wt0=buf(bf16, 256, 256), wt1=buf(bf16, 512, 256), sums=buf(f32, 18, 8, 128), vec=buf(f32, 80, 128),
         rows_e=buf(f32, 4, BLOCKS, crops, 128), rows_c=buf(f32, 2, BLOCKS, crops, 128),
         keys=buf(f32, devices * 16, 128), embed=buf(f32, 16, 128),
-        lower=[buf(f32, lows, n, 128) for n in TURN_ROWS], upper=[buf(f32, highs, n, 128) for n in TURN_ROWS],
+        moved=[[buf(f32, 1 << width, n, 128) for width in widths] for n in TURN_ROWS],
         key_load=dma(2 * micros), query_load=dma(micros, 2), store=dma(micros, images + 1),
-        low_send=dma(3, lows), low_recv=dma(3, lows), high_send=dma(3, highs), high_recv=dma(3, highs),
-        key_send=dma(devices), key_recv=dma(devices),
+        move_send=dma(3, 3, 1 << widths[0]), move_recv=dma(3, 3, 1 << widths[0]),
+        key_send=dma(3, 1 << widths[0]), key_recv=dma(3, 1 << widths[0]),
     )
     first, second, third, fourth = (buf(bf16, *shape) for shape in weights)
     scratch |= dict(w1q=first, w2q=second, w3q=third, w4q=fourth, w1k=first, w2k=second, w3k=third, w4k=fourth)
+    wires = (bf16, bf16, f32)
     if own:
         scratch |= {n: buf(f32, *shape) for n, shape in totals.items()}
         scratch |= dict(
-            sent=buf(bf16, 2, PACK, 128), swapped_in=buf(bf16, 2, PACK, 128), gathered=buf(bf16, 2, chips, PACK, 128),
-            parts=buf(f32, 3, 2, chips, JOB, 128), arrived=buf(f32, 3, chips, JOB, 128),
-            sending=buf(bf16, 3, chips, JOB, 128), landed=buf(bf16, 3, chips, JOB, 128),
-            core_send=dma(2), core_recv=dma(2), wide_send=dma(2, chips), wide_recv=dma(2, chips),
-            join_send=dma(2), join_recv=dma(2), swap_send=dma(3), swap_recv=dma(3),
-            row_send=dma(3, chips), row_recv=dma(3, chips), result_send=dma(3), result_recv=dma(3),
+            sent=buf(bf16, 2, PACK, 128), gathered=buf(bf16, 2, 2, 4, 4, PACK, 128),
+            parts=[buf(f32, 2, 4, 4, n, 128) for n in JOB_ROWS], arrived=[buf(f32, 4, 4, n, 128) for n in JOB_ROWS],
+            plane_out=[buf(t, 4, 4, n, 128) for n, t in zip(JOB_ROWS, wires)],
+            plane_in=[buf(t, 4, 4, n, 128) for n, t in zip(JOB_ROWS, wires)],
+            column_out=[buf(t, 4, n, 128) for n, t in zip(JOB_ROWS, wires)],
+            column_in=[buf(t, 4, n, 128) for n, t in zip(JOB_ROWS, wires)],
+            gather_send=dma(2, 3, 3), gather_recv=dma(2, 3, 3), sum_send=dma(3, 3, 4), sum_recv=dma(3, 3, 4),
         )
     names = list(inputs) + list(outputs) + list(scratch)
     out = pl.pallas_call(
@@ -1102,35 +1115,31 @@
     return types.SimpleNamespace(**dict(zip(outputs, out)))
 
 
-def finish_kernel(device, packed, loss, reduce_out, spatial_out, expand_out, shortcut_out, gains, shifts):
-    here = lax.rem(device[0], 2) == 0
-    reduce_out[...] = jnp.where(here, packed[2, 0, 0:16, 0:64], packed[2, 0, 0:16, 64:128])
-    rows = jnp.concatenate([packed[1, 0], packed[1, 1, 0:24], jnp.zeros((56, 128), f32)], axis=0).T
-    spatial_out[...] = jnp.where(here, rows[0:64, 0:72], rows[64:128, 0:72])
-    shortcut = [packed[0, 0, 32:48]] + [packed[0, 1, k * 16 : (k + 1) * 16] for k in range(3)]
+def finish_kernel(packed, loss, reduce_out, spatial_out, expand_out, shortcut_out, gains, shifts):
+    reduce_out[0:8] = packed[96:104, 0:64]
+    reduce_out[8:16] = packed[96:104, 64:128]
+    rows = jnp.concatenate([packed[48:88], jnp.zeros((88, 128), f32)], axis=0).T
+    spatial_out[...] = jnp.concatenate([rows[0:64, 0:40], rows[64:128, 0:32]], axis=1)
     for block in range(2):
         lanes = slice(block * 128, (block + 1) * 128)
-        first, second = block, block + 2
-        expand_out[:, lanes] = jnp.where(
-            here, packed[0, 0, first * 8 : first * 8 + 8], packed[0, 0, second * 8 : second * 8 + 8])
-        shortcut_out[:, lanes] = jnp.where(here, shortcut[first], shortcut[second])
-    for half, ref in enumerate((gains, shifts)):
-        for row in range(NORMS // 128):
-            ref[pl.ds(row * 128, 128)] = packed[2, half, 16 + row] + packed[2, half, 32 + row]
-    loss[...] = packed[2, 0, 26:27, 0:1] + packed[2, 0, 42:43, 0:1]
-
-
-def finish_pass(device, packed):
+        expand_out[:, lanes] = packed[block * 8 : block * 8 + 8]
+        shortcut_out[:, lanes] = packed[16 + block * 16 : 32 + block * 16]
+    for row in range(NORMS // 128):
+        gains[pl.ds(row * 128, 128)] = packed[104 + row]
+        shifts[pl.ds(row * 128, 128)] = packed[116 + row]
+    loss[...] = packed[114:115, 0:1]
+
+
+def finish_pass(packed):
     vmem = pl.BlockSpec(memory_space=pltpu.VMEM)
-    smem = pl.BlockSpec(memory_space=pltpu.SMEM)
     shapes = [(1, 1), (16, 64), (64, 72), (8, 256), (16, 256), (NORMS,), (NORMS,)]
     return pl.pallas_call(
         finish_kernel,
         out_shape=[jax.ShapeDtypeStruct(shape, f32) for shape in shapes],
-        in_specs=[smem, vmem],
+        in_specs=[vmem],
         out_specs=[vmem] * 7,
         name="finish",
-    )(device, packed)
+    )(packed)
 
 
 def gather_weights(shards):
@@ -1159,8 +1168,7 @@
     )
     fields = (out.big_out.reshape(query_global.shape), out.small_out.reshape(small_crop_query.shape))
     if own:
-        device = (lax.axis_index("dp") * cores + lax.axis_index("fsdp")).astype(jnp.int32).reshape(1)
-        loss, first, second, third, fourth, gains_grad, shifts_grad = finish_pass(device, out.packed)
+        loss, first, second, third, fourth, gains_grad, shifts_grad = finish_pass(out.packed)
         return (loss.reshape(()), *fields, first, second.T, third, fourth, gains_grad, shifts_grad)
     totals = (out.g1.T, out.g2.T, out.g3, out.g4)
     summed = lax.psum_scatter(totals, "dp", scatter_dimension=0, tiled=True)

time: 141 us -> 158 us (1.12)
  Pallas kernels: 132 us -> 149 us
    pallas_call x1, Pallas kernels: 130 us -> 148 us  [step_pass(): pl.pallas_call(functools.partial(step_kernel, axes, own, slots, names), o...]
where the time goes in v1:
time: 158 us
  Pallas kernels  149 us (94%)
  local copies, waits for them, and re-layouts  7.93 us (5%)
    pallas_call x1, Pallas kernels, step_pass(): pl.pallas_call(functools.partial(step_kernel, axes, own, slots, names), o...  148 us
    unnamed x4, local copies, waits for them, and re-layouts  7.93 us

profile of v1, /device:TPU:0, one launch (start us, length us, event | category | flops | bytes accessed | tf_op | source)
XLA Modules:
  0.0 157.9 jit_solution(11773554182362148479)
XLA Ops:
  0.6 147.7 %step.1 = (bf16[2,6272,256]{2,1,0:T(8,128)(2,1)}, bf16[2,3456,256]{2,1,0:T(8,128)(2,1)}, f32[128,128]{1,0:T(8,128)}) custom-call(bf16[2,6272,256]{2,1,0:T(8,128)(2,1)} %bitcast.9, bf16[2,3456,256]{2,1,0:T(8,128)(2,1)} %bitcast.12, bf16[2,6272,256]{2,1,0:T(8,128)(2,1)} %bitcast.10, s32[2,2]{1,0:T(2,128)} %refs_3_.1, s32[2,2]{1,0:T(2,128)} %refs_4_.1, ...), custom_call_target="tpu_custom_call" | custom-call | tf_op jit(solution)/shard_map/step/pallas_call | solution.py:1106
  148.3 1.6 %finish.1 = (f32[1,1]{1,0:T(1,128)}, f32[16,64]{1,0:T(8,128)}, f32[64,72]{1,0:T(8,128)}, f32[8,256]{1,0:T(8,128)}, f32[16,256]{1,0:T(8,128)}, /*index=5*/f32[1280]{0:T(1024)}, f32[1280]{0:T(1024)}) custom-call(f32[128,128]{1,0:T(8,128)} %get-tuple-element.19.packed), custom_call_target="tpu_custom_call" | custom-call | tf_op jit(solution)/shard_map/finish/pallas_call | solution.py:1136
  149.9 0.0 copy-start
  149.9 6.1 %copy.28 = bf16[2,2,56,56,256]{4,3,2,1,0:T(8,128)(2,1)} copy(bf16[2,2,56,56,256]{4,3,2,1,0:T(8,128)(2,1)} %bitcast.11) | data formatting | bytes 12845056
  156.1 0.0 copy-done
  156.1 1.8 %copy.29 = bf16[2,2,3,24,24,256]{5,4,3,2,1,0:T(8,128)(2,1)} copy(bf16[2,2,3,24,24,256]{5,4,3,2,1,0:T(8,128)(2,1)S(1)} %bitcast.13) | data formatting | bytes 7077888
Async XLA Ops:
  149.9 6.1 %copy-start = (bf16[2,3456,256]{2,1,0:T(8,128)(2,1)S(1)}, bf16[2,3456,256]{2,1,0:T(8,128)(2,1)}, u32[]{:S(2)}) copy-start(bf16[2,3456,256]{2,1,0:T(8,128)(2,1)} %get-tuple-element.22) | copy-start | bytes 10616836

commit v2 on v1

--- a/solution.py
+++ b/solution.py
@@ -63,8 +63,8 @@
 MOMENTUM = 0.999
 MESH = pl.DeviceIdType.MESH
 PACK = 96
-JOB_ROWS = (48, 48, 32)
-TURN_ROWS = (48, 16, 32)
+JOB_ROWS = (48, 48, 24, 8)
+TURN_ROWS = (24, 8, 16)
 
 
 def line(vector, start):
@@ -178,7 +178,7 @@
 
 def stage_widths(devices):
     bits = devices.bit_length() - 1
-    return (bits + 2) // 3, (bits + 1) // 3, bits // 3
+    return (bits + 1) // 2, bits // 2
 
 
 def step_kernel(axes, own, slots, names, *refs):
@@ -186,7 +186,7 @@
     chips, cores = axes
     devices = chips * cores
     widths = stage_widths(devices)
-    shifts_of = (0, widths[0], widths[0] + widths[1])
+    shifts_of = (0, widths[0])
     counts, mask = r.counts, r.mask
     micros, images = counts.shape
     fields = field_pair(images, slots)
@@ -275,11 +275,11 @@
 
     moved = r.moved
 
-    def exchange_copies(turn, stage):
-        ref = moved[turn][stage]
+    def exchange_copies(m, turn, stage):
+        ref, which = moved[m * 3 + turn][stage], m * 3 + turn
         return [
             remote(
-                ref.at[0], ref.at[k], r.move_send.at[turn, stage, k], r.move_recv.at[turn, stage, k],
+                ref.at[0], ref.at[k], r.move_send.at[which, stage, k], r.move_recv.at[which, stage, k],
                 partner(k << shifts_of[stage]))
             for k in range(1, 1 << widths[stage])
         ]
@@ -287,35 +287,33 @@
     def picked(m, stage):
         return lax.rem(lax.div(jnp.bitwise_xor(mask[m, 0], mask[m, 1]), 1 << shifts_of[stage]), 1 << widths[stage])
 
-    def exchange_start(turn):
-        for copy in exchange_copies(turn, 0):
+    def exchange_start(m, turn):
+        for copy in exchange_copies(m, turn, 0):
             copy.start()
 
-    def exchange_next(turn, stage):
-        for copy in exchange_copies(turn, stage - 1):
+    def exchange_next(m, turn):
+        for copy in exchange_copies(m, turn, 0):
             copy.wait()
-        half = TURN_ROWS[turn] // micros
-        for m in range(micros):
-            rows = slice(m * half, (m + 1) * half)
-            moved[turn][stage][0, rows] = moved[turn][stage - 1][picked(m, stage - 1), rows]
-        for copy in exchange_copies(turn, stage):
+        first, second = moved[m * 3 + turn]
+        second[0] = first[picked(m, 0)]
+        for copy in exchange_copies(m, turn, 1):
             copy.start()
 
-    def exchange_end(turn):
-        for copy in exchange_copies(turn, 2):
+    def exchange_end(m, turn):
+        for copy in exchange_copies(m, turn, 1):
             copy.wait()
 
-    def put_moments(turn, row, start, size, step):
+    def put_moments(m, turn, row, start, size, step):
         pivot = folded(wide[at(start, step, 8)]).sum(0, keepdims=True) / step
         total, square = moments(wide, start, size, step, pivot)
         off = total.sum(0, keepdims=True) / size
-        moved[turn][0][0, pl.ds(row, 1)] = pivot + off
-        moved[turn][0][0, pl.ds(row + 1, 1)] = jnp.maximum(square.sum(0, keepdims=True) - off * off * size, 0.0)
-
-    def combined(turn, m, row, other, count):
-        pick = picked(m, 2)
-        mean, spread = moved[turn][0][0, pl.ds(row, 1)], moved[turn][0][0, pl.ds(row + 1, 1)]
-        mean2, spread2 = moved[turn][2][pick, pl.ds(other, 1)], moved[turn][2][pick, pl.ds(other + 1, 1)]
+        moved[m * 3 + turn][0][0, pl.ds(row, 1)] = pivot + off
+        moved[m * 3 + turn][0][0, pl.ds(row + 1, 1)] = jnp.maximum(square.sum(0, keepdims=True) - off * off * size, 0.0)
+
+    def combined(m, turn, row, other, count):
+        pick = picked(m, 1)
+        mean, spread = moved[m * 3 + turn][0][0, pl.ds(row, 1)], moved[m * 3 + turn][0][0, pl.ds(row + 1, 1)]
+        mean2, spread2 = moved[m * 3 + turn][1][pick, pl.ds(other, 1)], moved[m * 3 + turn][1][pick, pl.ds(other + 1, 1)]
         apart = mean - mean2
         variance = (spread + spread2 + apart * apart * (count * 0.5)) / (2.0 * count)
         return (mean + mean2) * 0.5, lax.rsqrt(variance + NORM_EPS)
@@ -348,19 +346,17 @@
         for block in range(BLOCKS):
             wide[at(start + block * big.out_area, big.out_area)] = value[:, block * 128 : (block + 1) * 128]
 
-    def key_a(i):
-        m, c = lax.div(i, 2), lax.rem(i, 2)
+    def key_a(m, c):
         start = m * first_row + c * big.area
-        wide[at(start, big.area)] = dot(field[at(key_base + i * big.area, big.area)], wk[0][...])
-        put_moments(0, m * 24 + c * 2, start, big.area, 112)
+        wide[at(start, big.area)] = dot(field[at(key_base + (2 * m + c) * big.area, big.area)], wk[0][...])
+        put_moments(m, 0, c * 2, start, big.area, 112)
         start = m * first_row + spare
-        key_side(i, start)
+        key_side(2 * m + c, start)
         for block in range(BLOCKS):
-            put_moments(0, m * 24 + 8 + (c * BLOCKS + block) * 2, start + block * big.out_area, big.out_area, 112)
-
-    def key_b(i):
-        m, c = lax.div(i, 2), lax.rem(i, 2)
-        scale, bias = affine(combined(0, m, m * 24 + c * 2, m * 24 + (1 - c) * 2, area), 0)
+            put_moments(m, 0, 8 + (c * BLOCKS + block) * 2, start + block * big.out_area, big.out_area, 112)
+
+    def key_b(m, c):
+        scale, bias = affine(combined(m, 0, c * 2, (1 - c) * 2, area), 0)
 
         def rows_of(y):
             for k in range(4):
@@ -373,30 +369,28 @@
         start = m * first_row + spare + c * big.out_area
         for k in range(big.half):
             wide[pl.ds(start + k * big.half, big.half)] = value[k * big.wide : k * big.wide + big.half]
-        put_moments(1, m * 8 + c * 2, start, big.out_area, 112)
-
-    def key_c(i):
-        m, c = lax.div(i, 2), lax.rem(i, 2)
-        scale, bias = affine(combined(1, m, m * 8 + c * 2, m * 8 + (1 - c) * 2, out_area), CMID)
+        put_moments(m, 1, c * 2, start, big.out_area, 112)
+
+    def key_c(m, c):
+        scale, bias = affine(combined(m, 1, c * 2, (1 - c) * 2, out_area), CMID)
         for k in range(big.out_area // 112):
             v = wide[at(m * first_row + spare + c * big.out_area + k * 112, 112)] * scale + bias
             thin[at(m * outs + c * big.out_area + k * 112, 112)] = gelu_only(v).astype(bf16)
         start = m * first_row
         key_third(m, c, start)
         for block in range(BLOCKS):
-            put_moments(2, m * 16 + (c * BLOCKS + block) * 2, start + block * big.out_area, big.out_area, 112)
-
-    def key_d(i):
-        m, c = lax.div(i, 2), lax.rem(i, 2)
+            put_moments(m, 2, (c * BLOCKS + block) * 2, start + block * big.out_area, big.out_area, 112)
+
+    def key_d(m, c):
         start = m * first_row
         key_third(m, c, start)
-        key_side(i, start + BLOCKS * big.out_area)
+        key_side(2 * m + c, start + BLOCKS * big.out_area)
         parts = []
         for block in range(BLOCKS):
             lanes = 2 * CMID + block * 128
             row, other = (c * BLOCKS + block) * 2, ((1 - c) * BLOCKS + block) * 2
-            scale3, bias3 = affine(combined(2, m, m * 16 + row, m * 16 + other, out_area), lanes)
-            scale4, bias4 = affine(combined(0, m, m * 24 + 8 + row, m * 24 + 8 + other, out_area), lanes + COUT)
+            scale3, bias3 = affine(combined(m, 2, row, other, out_area), lanes)
+            scale4, bias4 = affine(combined(m, 0, 8 + row, 8 + other, out_area), lanes + COUT)
             bias = bias3 + bias4
             e = jnp.zeros((8, 128), f32)
             for k in range(big.out_area // 112):
@@ -409,89 +403,59 @@
         for block in range(BLOCKS):
             r.embed[pl.ds(m * 8 + c * BLOCKS + block, 1)] = parts[block] * inverse
 
-    def share_copies(stage):
-        size = 16 << shifts_of[stage]
-        here = keys.at[pl.ds(pl.multiple_of(lax.div(me, 1 << shifts_of[stage]) * size, 16), size)]
-        return [
-            remote(here, here, r.key_send.at[stage, k], r.key_recv.at[stage, k], partner(k << shifts_of[stage]))
-            for k in range(1, 1 << widths[stage])
-        ]
-
-    def share_start(stage):
-        if stage == 0:
-            keys[at(me * 16, 16)] = r.embed[...]
-        for copy in share_copies(stage):
-            copy.start()
-
-    def share_end(stage):
-        for copy in share_copies(stage):
-            copy.wait()
+    def key_copy(m, k):
+        mine = keys.at[pl.ds(pl.multiple_of((m * devices + me) * 8, 8), 8)]
+        return remote(
+            r.embed.at[pl.ds(m * 8, 8)], mine, r.key_send.at[m, k], r.key_recv.at[m, k], place(lax.rem(me + k, devices)))
+
+    def share_start(m):
+        keys[at((m * devices + me) * 8, 8, 8)] = r.embed[m * 8 : (m + 1) * 8]
+        repeat(1, devices, lambda k: key_copy(m, k).start())
+
+    def share_end(m):
+        repeat(1, devices, lambda k: key_copy(m, k).wait())
 
     def core_copy(job):
+        return remote(r.parts[job].at[1 - core], r.arrived[job], r.core_send.at[job], r.core_recv.at[job], partner(1))
+
+    def row_copy(job, target, source):
         return remote(
-            r.parts[job].at[1 - core], r.arrived[job], r.sum_send.at[job, 0, 0], r.sum_recv.at[job, 0, 0], partner(1))
-
-    def plane_copies(job):
-        return [
-            remote(
-                r.plane_out[job].at[k], r.plane_in[job].at[k], r.sum_send.at[job, 1, k], r.sum_recv.at[job, 1, k],
-                partner(2 * k))
-            for k in range(1, 4)
-        ]
-
-    def column_copies(job):
-        return [
-            remote(
-                r.column_out[job].at[k], r.column_in[job].at[k], r.sum_send.at[job, 2, k], r.sum_recv.at[job, 2, k],
-                partner(8 * k))
-            for k in range(1, 4)
-        ]
-
-    def job_plane(job):
+            r.outward[job].at[target], r.inward[job].at[source], r.row_send.at[job, target], r.row_recv.at[job, source],
+            (target, core))
+
+    def job_send(job):
         core_copy(job).wait()
-        own_part, wire = r.parts[job], r.plane_out[job].dtype
-        for k in range(1, 4):
-            far = flipped(xy, k)
-            r.plane_out[job][k] = (own_part[core, far] + r.arrived[job][far]).astype(wire)
-        for copy in plane_copies(job):
-            copy.start()
-        r.arrived[job][xy] = own_part[core, xy] + r.arrived[job][xy]
-
-    def job_column(job):
-        for copy in plane_copies(job):
-            copy.wait()
-        held, wire = r.arrived[job], r.column_out[job].dtype
-        for far in range(4):
-            held[xy, far] += sum(r.plane_in[job][k, far].astype(f32) for k in range(1, 4))
-        for k in range(1, 4):
-            r.column_out[job][k] = held[xy, flipped(z, k)].astype(wire)
-        for copy in column_copies(job):
-            copy.start()
+
+        def turn(k):
+            target = lax.rem(chip + k, chips)
+            value = r.parts[job][core, target] + r.arrived[job][target]
+            r.outward[job][target] = value.astype(r.outward[job].dtype)
+            row_copy(job, target, chip).start()
+
+        repeat(1, chips, turn)
 
     def job_end(job):
-        for copy in column_copies(job):
-            copy.wait()
+        def add(k, total):
+            source = lax.rem(chip + chips - k, chips)
+            row_copy(job, source, source).wait_recv()
+            return total + r.inward[job][source].astype(f32)
+
+        total = lax.fori_loop(1, chips, add, r.parts[job][core, chip] + r.arrived[job][chip])
         start = sum(JOB_ROWS[:job])
-        total = r.arrived[job][xy, z] + sum(r.column_in[job][k].astype(f32) for k in range(1, 4))
         r.packed[start : start + JOB_ROWS[job]] = total
-
-    def each_chip(body):
-        def turn(i):
-            body(i, lax.rem(i, 4), lax.div(i, 4))
-
-        repeat(0, chips, turn)
+        repeat(1, chips, lambda k: row_copy(job, lax.rem(chip + k, chips), chip).wait_send())
 
     def fill_head():
         part, third, fourth = r.parts[0], grads[2], grads[3]
 
-        def turn(i, to_xy, to_z):
+        def turn(i):
             for block in range(BLOCKS):
                 half, row = block // 2, block % 2
                 lanes = slice(block * 128, (block + 1) * 128)
-                part[half, to_xy, to_z, row * 8 : row * 8 + 8] = third[at(i * 8, 8, 8), lanes]
-                part[half, to_xy, to_z, 16 + row * 16 : 32 + row * 16] = fourth[at(i * 16, 16), lanes]
-
-        each_chip(turn)
+                part[half, i, row * 8 : row * 8 + 8] = third[at(i * 8, 8, 8), lanes]
+                part[half, i, 16 + row * 16 : 32 + row * 16] = fourth[at(i * 16, 16), lanes]
+
+        repeat(0, chips, turn)
         core_copy(0).start()
 
     def fill_spatial():
@@ -501,21 +465,18 @@
             gy2[lanes] = grads[1][:, lanes].T
         filler = jnp.zeros((8, 128), f32)
 
-        def turn(i, to_xy, to_z):
+        def turn(i):
             top = gy2[at(i * 72, 40, 8)]
             bottom = jnp.concatenate([gy2[at(i * 72 + 40, 32, 8)], filler], axis=0)
             for half in range(2):
-                part[half, to_xy, to_z, 0:40] = side_by_side(top, bottom, half)
-                part[half, to_xy, to_z, 40:48] = filler
-
-        each_chip(turn)
+                part[half, i, 0:40] = side_by_side(top, bottom, half)
+                part[half, i, 40:48] = filler
+
+        repeat(0, chips, turn)
         core_copy(1).start()
 
-    def fill_rest():
+    def fill_sums():
         part = r.parts[2]
-        for tile in range(2):
-            lanes = slice(tile * 128, (tile + 1) * 128)
-            gy2[lanes] = grads[0][:, lanes].T
         column = lax.broadcasted_iota(jnp.int32, (1, 128), 1)
         filler = jnp.zeros((1, 128), f32)
         rows = [gain_sum[:, k * 128 : (k + 1) * 128] for k in range(10)]
@@ -523,22 +484,31 @@
         rows += [shift_sum[:, k * 128 : (k + 1) * 128] for k in range(10)] + [filler, filler]
         rows = jnp.concatenate(rows, axis=0)
 
-        def turn(i, to_xy, to_z):
+        def turn(i):
             for half in range(2):
-                value = side_by_side(gy2[at(i * 16, 8, 8)], gy2[at(i * 16 + 8, 8, 8)], half)
-                part[half, to_xy, to_z] = jnp.concatenate([value, rows], axis=0)
-
-        each_chip(turn)
+                part[half, i] = rows
+
+        repeat(0, chips, turn)
         core_copy(2).start()
+
+    def fill_reduce():
+        part = r.parts[3]
+        for tile in range(2):
+            lanes = slice(tile * 128, (tile + 1) * 128)
+            gy2[lanes] = grads[0][:, lanes].T
+
+        def turn(i):
+            for half in range(2):
+                part[half, i] = side_by_side(gy2[at(i * 16, 8, 8)], gy2[at(i * 16 + 8, 8, 8)], half)
+
+        repeat(0, chips, turn)
+        core_copy(3).start()
 
     for load in query_loads(0) + key_loads:
         load.start()
-    flips = {k << shift for width, shift in zip(widths, shifts_of) for k in range(1, 1 << width)}
-    if own:
-        flips |= {1} | {2 * k for k in range(1, 4)} | {8 * k for k in range(1, 4)}
     barrier = pltpu.get_barrier_semaphore()
-    for flip in sorted(flips):
-        pl.semaphore_signal(barrier, inc=1, device_id=partner(flip), device_id_type=MESH)
+    repeat(1, devices, lambda k: pl.semaphore_signal(
+        barrier, inc=1, device_id=place(lax.rem(me + k, devices)), device_id_type=MESH))
     if own:
         current = [r.r0[...], r.s0[...], r.e0[...], r.p0[...]]
         lagged = [r.r1[...], r.s1[...], r.e1[...], r.p1[...]]
@@ -549,18 +519,17 @@
     else:
         for shard, w in zip((r.r0, r.s0, r.e0, r.p0, r.r1, r.s1, r.e1, r.p1), wq + wk):
             w[...] = shard[...]
-    if flips:
-        pl.semaphore_wait(barrier, len(flips))
+    if devices > 1:
+        pl.semaphore_wait(barrier, devices - 1)
     if own:
-        for which in range(2):
-            gather_start(which, 0)
+        gather_start(0, 0)
     for ref in list(planes_of.values()) + list(back_of.values()) + list(stage_of.values()) + grads + [
-        r.raised, gain_sum, shift_sum, loss_sum, gy2, moved[0][0], moved[1][0], moved[2][0]]:
+        r.raised, gain_sum, shift_sum, loss_sum, gy2] + [pair[0] for pair in moved]:
         ref[...] = jnp.zeros_like(ref)
     if own:
-        for which in range(2):
-            gather_end(which, 0)
-            gather_start(which, 1)
+        gather_end(0, 0)
+        gather_start(0, 1)
+        gather_start(1, 0)
 
     def micro_step(m):
         opening, closing = m == 0, m == micros - 1
@@ -630,12 +599,17 @@
             if own:
                 gather_end(0, 1)
                 gather_start(0, 2)
+                gather_end(1, 0)
+                gather_start(1, 1)
+                gather_end(0, 2)
+                unpacked(r.gathered, 0, chips, wk, gy2)
+            repeat(0, 2, lambda c: key_a(0, c))
+            exchange_start(0, 0)
+            if own:
                 gather_end(1, 1)
                 gather_start(1, 2)
-                gather_end(0, 2)
-                unpacked(r.gathered, 0, chips, wk, gy2)
-            repeat(0, 2 * micros, key_a)
-            exchange_start(0)
+            repeat(0, 2, lambda c: key_a(1, c))
+            exchange_start(1, 0)
             for load in query_loads(1):
                 load.start()
             if own:
@@ -669,7 +643,7 @@
             a1[at(start, size)] = dot(field[at(base + start, size)], w1[...])
             add_moments(a1, 0, kind, first, count, kind.row, kind.area, 0, 0, 784)
 
-        over_big(reduce_batch, (opening, lambda: exchange_next(0, 1)), (opening, lambda: exchange_next(0, 2)))
+        over_big(reduce_batch, (opening, lambda: exchange_next(0, 0)), (opening, lambda: exchange_next(1, 0)))
         over_small(reduce_batch)
         mean1, root1 = closed(sums[0], sums[1], vec[0:1], count1)
         scale1 = root1 * line(gains, 0)
@@ -678,9 +652,10 @@
 
         @pl.when(opening)
         def _():
-            exchange_end(0)
-            repeat(0, 2 * micros, key_b)
-            exchange_start(1)
+            for k in range(2):
+                exchange_end(k, 0)
+                repeat(0, 2, lambda c: key_b(k, c))
+                exchange_start(k, 1)
 
         sums[...] = jnp.zeros_like(sums)
 
@@ -694,14 +669,15 @@
                     slope1[at(start, 2 * kind.side)] = slope.astype(bf16)
                     split_planes(hidden, stage_of[kind.ahead], planes_of[kind.ahead], kind, first + c, k, k % 2)
 
-        over_big(hidden_batch, (opening, lambda: exchange_next(1, 1)), (opening, lambda: exchange_next(1, 2)))
+        over_big(hidden_batch, (opening, lambda: exchange_next(0, 1)), (opening, lambda: exchange_next(1, 1)))
         over_small(hidden_batch)
 
         @pl.when(opening)
         def _():
-            exchange_end(1)
-            repeat(0, 2 * micros, key_c)
-            exchange_start(2)
+            for k in range(2):
+                exchange_end(k, 1)
+                repeat(0, 2, lambda c: key_c(k, c))
+                exchange_start(k, 2)
 
         def spatial_batch(kind, first, count):
             half, lanes = kind.half, kind.wide
@@ -711,7 +687,7 @@
                 a2[pl.ds(start + k * half, half)] = value[k * lanes : k * lanes + half]
             add_moments(a2, 0, kind, first, count, kind.out_row, kind.out_area, 0, 16, 784)
 
-        over_big(spatial_batch, (opening, lambda: exchange_next(2, 1)), (opening, lambda: exchange_next(2, 2)))
+        over_big(spatial_batch, (opening, lambda: exchange_next(0, 2)), (opening, lambda: exchange_next(1, 2)))
         over_small(spatial_batch)
         mean2, root2 = closed(sums[16], sums[17], vec[0:1], count2)
         scale2 = root2 * line(gains, CMID)
@@ -720,9 +696,10 @@
 
         @pl.when(opening)
         def _():
-            exchange_end(2)
-            repeat(0, 2 * micros, key_d)
-            share_start(0)
+            for k in range(2):
+                exchange_end(k, 2)
+                repeat(0, 2, lambda c: key_d(k, c))
+                share_start(k)
 
         def head_product(which, source, weight, kind, first, count):
             start = kind.out_row + first * kind.out_area
@@ -748,17 +725,8 @@
                 thin[at(SLOPE2 + start + k * step, step)] = slope.astype(bf16)
             head_product(0, thin[at(H2 + start, size)], w3, kind, first, count)
 
-        def share_next(stage):
-            share_end(stage - 1)
-            share_start(stage)
-
-        over_big(expand_batch, (opening, lambda: None), (opening, lambda: share_next(1)))
+        over_big(expand_batch)
         over_small(expand_batch)
-
-        @pl.when(opening)
-        def _():
-            share_next(2)
-
         for which in range(2):
             for block in range(BLOCKS):
                 row = which * 4 + block
@@ -802,9 +770,7 @@
         over_big(embed_batch)
         over_small(embed_batch)
 
-        @pl.when(opening)
-        def _():
-            share_end(2)
+        share_end(m)
 
         def joined(which):
             return jnp.concatenate([rows_e[which, block] for block in range(BLOCKS)], axis=1)
@@ -823,7 +789,7 @@
         embedding = e * inverse
         key_blocks = [
             jnp.concatenate(
-                [keys[pl.ds(m * 8 + c * BLOCKS + block, devices, stride=16)] for c in range(images)], axis=0)
+                [keys[pl.ds(m * devices * 8 + c * BLOCKS + block, devices, stride=8)] for c in range(images)], axis=0)
             for block in range(BLOCKS)
         ]
         logits = sum(
@@ -960,10 +926,13 @@
             sums[0] += level
             sums[1] += reach
 
-        def job_hooks(job):
-            return ((closing, lambda: job_plane(job)), (closing, lambda: job_column(job))) if own else ()
-
-        over_big(spatial_back, *job_hooks(0))
+        def job_hooks(*jobs):
+            def sends(some):
+                return lambda: [job_send(job) for job in some]
+
+            return [(closing, sends(some)) for some in jobs] if own else []
+
+        over_big(spatial_back, *job_hooks((0,)))
         over_small(spatial_back)
         norm_back(1, slice(0, CMID), count1)
 
@@ -972,7 +941,7 @@
             @pl.when(closing)
             def _():
                 fill_spatial()
-                job_end(0)
+                fill_sums()
 
         def reduce_back(kind, first, count):
             step = step_of(kind)
@@ -988,15 +957,15 @@
                     slope1[here] = grad.astype(bf16)
             grads[0][...] += dot_rows(slope1[at(start, size)], field[at(base + start, size)])
 
-        over_big(reduce_back, *job_hooks(1))
+        over_big(reduce_back, *job_hooks((1,), (2,)))
         over_small(reduce_back)
 
         if own:
 
             @pl.when(closing)
             def _():
-                fill_rest()
-                job_end(1)
+                fill_reduce()
+                job_end(0)
 
         raised = r.raised
 
@@ -1020,12 +989,13 @@
             else:
                 store_small(m).start()
 
-        over_big(field_back, *job_hooks(2))
+        over_big(field_back, *job_hooks((), (3,)))
         over_small(field_back)
 
     repeat(0, micros, micro_step)
     if own:
-        job_end(2)
+        for job in range(1, 4):
+            job_end(job)
     for m in range(micros):
         for c in range(images):
             store_big(m, c).wait()
@@ -1083,24 +1053,23 @@
         wt0=buf(bf16, 256, 256), wt1=buf(bf16, 512, 256), sums=buf(f32, 18, 8, 128), vec=buf(f32, 80, 128),
         rows_e=buf(f32, 4, BLOCKS, crops, 128), rows_c=buf(f32, 2, BLOCKS, crops, 128),
         keys=buf(f32, devices * 16, 128), embed=buf(f32, 16, 128),
-        moved=[[buf(f32, 1 << width, n, 128) for width in widths] for n in TURN_ROWS],
+        moved=[[buf(f32, 1 << width, n, 128) for width in widths] for _ in range(micros) for n in TURN_ROWS],
         key_load=dma(2 * micros), query_load=dma(micros, 2), store=dma(micros, images + 1),
-        move_send=dma(3, 3, 1 << widths[0]), move_recv=dma(3, 3, 1 << widths[0]),
-        key_send=dma(3, 1 << widths[0]), key_recv=dma(3, 1 << widths[0]),
+        move_send=dma(3 * micros, 2, 1 << widths[0]), move_recv=dma(3 * micros, 2, 1 << widths[0]),
+        key_send=dma(micros, devices), key_recv=dma(micros, devices),
     )
     first, second, third, fourth = (buf(bf16, *shape) for shape in weights)
     scratch |= dict(w1q=first, w2q=second, w3q=third, w4q=fourth, w1k=first, w2k=second, w3k=third, w4k=fourth)
-    wires = (bf16, bf16, f32)
+    wires = (bf16, bf16, f32, f32)
     if own:
         scratch |= {n: buf(f32, *shape) for n, shape in totals.items()}
         scratch |= dict(
             sent=buf(bf16, 2, PACK, 128), gathered=buf(bf16, 2, 2, 4, 4, PACK, 128),
-            parts=[buf(f32, 2, 4, 4, n, 128) for n in JOB_ROWS], arrived=[buf(f32, 4, 4, n, 128) for n in JOB_ROWS],
-            plane_out=[buf(t, 4, 4, n, 128) for n, t in zip(JOB_ROWS, wires)],
-            plane_in=[buf(t, 4, 4, n, 128) for n, t in zip(JOB_ROWS, wires)],
-            column_out=[buf(t, 4, n, 128) for n, t in zip(JOB_ROWS, wires)],
-            column_in=[buf(t, 4, n, 128) for n, t in zip(JOB_ROWS, wires)],
-            gather_send=dma(2, 3, 3), gather_recv=dma(2, 3, 3), sum_send=dma(3, 3, 4), sum_recv=dma(3, 3, 4),
+            parts=[buf(f32, 2, chips, n, 128) for n in JOB_ROWS], arrived=[buf(f32, chips, n, 128) for n in JOB_ROWS],
+            outward=[buf(t, chips, n, 128) for n, t in zip(JOB_ROWS, wires)],
+            inward=[buf(t, chips, n, 128) for n, t in zip(JOB_ROWS, wires)],
+            gather_send=dma(2, 3, 3), gather_recv=dma(2, 3, 3), core_send=dma(4), core_recv=dma(4),
+            row_send=dma(4, chips), row_recv=dma(4, chips),
         )
     names = list(inputs) + list(outputs) + list(scratch)
     out = pl.pallas_call(
@@ -1116,8 +1085,8 @@
 
 
 def finish_kernel(packed, loss, reduce_out, spatial_out, expand_out, shortcut_out, gains, shifts):
-    reduce_out[0:8] = packed[96:104, 0:64]
-    reduce_out[8:16] = packed[96:104, 64:128]
+    reduce_out[0:8] = packed[120:128, 0:64]
+    reduce_out[8:16] = packed[120:128, 64:128]
     rows = jnp.concatenate([packed[48:88], jnp.zeros((88, 128), f32)], axis=0).T
     spatial_out[...] = jnp.concatenate([rows[0:64, 0:40], rows[64:128, 0:32]], axis=1)
     for block in range(2):
@@ -1125,9 +1094,9 @@
         expand_out[:, lanes] = packed[block * 8 : block * 8 + 8]
         shortcut_out[:, lanes] = packed[16 + block * 16 : 32 + block * 16]
     for row in range(NORMS // 128):
-        gains[pl.ds(row * 128, 128)] = packed[104 + row]
-        shifts[pl.ds(row * 128, 128)] = packed[116 + row]
-    loss[...] = packed[114:115, 0:1]
+        gains[pl.ds(row * 128, 128)] = packed[96 + row]
+        shifts[pl.ds(row * 128, 128)] = packed[108 + row]
+    loss[...] = packed[106:107, 0:1]
 
 
 def finish_pass(packed):

time: 158 us -> 137 us (0.87)
  Pallas kernels: 149 us -> 128 us
    pallas_call x1, Pallas kernels: 148 us -> 127 us  [step_pass(): pl.pallas_call(functools.partial(step_kernel, axes, own, slots, names), o...]
where the time goes in v2:
time: 137 us
  Pallas kernels  128 us (93%)
  local copies, waits for them, and re-layouts  7.93 us (6%)
    pallas_call x1, Pallas kernels, step_pass(): pl.pallas_call(functools.partial(step_kernel, axes, own, slots, names), o...  127 us
    unnamed x4, local copies, waits for them, and re-layouts  7.93 us

profile of v2, /device:TPU:0, one launch (start us, length us, event | category | flops | bytes accessed | tf_op | source)
XLA Modules:
  0.0 136.8 jit_solution(9980284556219804550)
XLA Ops:
  0.6 126.6 %step.1 = (bf16[2,6272,256]{2,1,0:T(8,128)(2,1)}, bf16[2,3456,256]{2,1,0:T(8,128)(2,1)}, f32[128,128]{1,0:T(8,128)}) custom-call(bf16[2,6272,256]{2,1,0:T(8,128)(2,1)} %bitcast.9, bf16[2,3456,256]{2,1,0:T(8,128)(2,1)} %bitcast.12, bf16[2,6272,256]{2,1,0:T(8,128)(2,1)} %bitcast.10, s32[2,2]{1,0:T(2,128)} %refs_3_.1, s32[2,2]{1,0:T(2,128)} %refs_4_.1, ...), custom_call_target="tpu_custom_call" | custom-call | tf_op jit(solution)/shard_map/step/pallas_call | solution.py:1075
  127.3 1.6 %finish.1 = (f32[1,1]{1,0:T(1,128)}, f32[16,64]{1,0:T(8,128)}, f32[64,72]{1,0:T(8,128)}, f32[8,256]{1,0:T(8,128)}, f32[16,256]{1,0:T(8,128)}, /*index=5*/f32[1280]{0:T(1024)}, f32[1280]{0:T(1024)}) custom-call(f32[128,128]{1,0:T(8,128)} %get-tuple-element.19.packed), custom_call_target="tpu_custom_call" | custom-call | tf_op jit(solution)/shard_map/finish/pallas_call | solution.py:1105
  128.9 0.0 copy-start
  128.9 6.1 %copy.28 = bf16[2,2,56,56,256]{4,3,2,1,0:T(8,128)(2,1)} copy(bf16[2,2,56,56,256]{4,3,2,1,0:T(8,128)(2,1)} %bitcast.11) | data formatting | bytes 12845056
  135.0 0.0 copy-done
  135.0 1.8 %copy.29 = bf16[2,2,3,24,24,256]{5,4,3,2,1,0:T(8,128)(2,1)} copy(bf16[2,2,3,24,24,256]{5,4,3,2,1,0:T(8,128)(2,1)S(1)} %bitcast.13) | data formatting | bytes 7077888
Async XLA Ops:
  128.9 6.1 %copy-start = (bf16[2,3456,256]{2,1,0:T(8,128)(2,1)S(1)}, bf16[2,3456,256]{2,1,0:T(8,128)(2,1)}, u32[]{:S(2)}) copy-start(bf16[2,3456,256]{2,1,0:T(8,128)(2,1)} %get-tuple-element.22) | copy-start | bytes 10616836

commit v3 on v2

--- a/solution.py
+++ b/solution.py
@@ -32,6 +32,8 @@
 
 
 def at(start, size, align=16):
+    if isinstance(start, int):
+        return pl.ds(start, size)
     return pl.ds(pl.multiple_of(start, align), size)
 
 
@@ -45,10 +47,6 @@
 
 def dot_rows(a, b):
     return lax.dot_general(a, b, (((0,), (0,)), ((), ())), preferred_element_type=f32)
-
-
-def dot_exact(a, b, dims):
-    return lax.dot_general(a, b, (dims, ((), ())), precision=lax.Precision.HIGHEST, preferred_element_type=f32)
 
 
 def gelu_pair(v):
@@ -69,6 +67,11 @@
 
 def line(vector, start):
     return vector[pl.ds(start, 128)].reshape(1, 128)
+
+
+def two_parts(x):
+    high = x.astype(bf16)
+    return high, (x - high.astype(f32)).astype(bf16)
 
 
 def moments(ref, start, size, step, pivot):
@@ -376,15 +379,15 @@
         for k in range(big.out_area // 112):
             v = wide[at(m * first_row + spare + c * big.out_area + k * 112, 112)] * scale + bias
             thin[at(m * outs + c * big.out_area + k * 112, 112)] = gelu_only(v).astype(bf16)
-        start = m * first_row
+        start = m * first_row + c * BLOCKS * big.out_area
         key_third(m, c, start)
         for block in range(BLOCKS):
             put_moments(m, 2, (c * BLOCKS + block) * 2, start + block * big.out_area, big.out_area, 112)
 
     def key_d(m, c):
-        start = m * first_row
-        key_third(m, c, start)
-        key_side(2 * m + c, start + BLOCKS * big.out_area)
+        start = m * first_row + c * BLOCKS * big.out_area
+        side = m * first_row + spare
+        key_side(2 * m + c, side)
         parts = []
         for block in range(BLOCKS):
             lanes = 2 * CMID + block * 128
@@ -395,7 +398,7 @@
             e = jnp.zeros((8, 128), f32)
             for k in range(big.out_area // 112):
                 x3 = wide[at(start + block * big.out_area + k * 112, 112)]
-                x4 = wide[at(start + (BLOCKS + block) * big.out_area + k * 112, 112)]
+                x4 = wide[at(side + block * big.out_area + k * 112, 112)]
                 e += folded(gelu_only(x3 * scale3 + x4 * scale4 + bias))
             parts.append(e.sum(0, keepdims=True) / out_area)
         length = sum(jnp.sum(part * part, axis=1, keepdims=True) for part in parts)
@@ -426,24 +429,22 @@
     def job_send(job):
         core_copy(job).wait()
 
-        def turn(k):
+        for k in range(1, chips):
             target = lax.rem(chip + k, chips)
             value = r.parts[job][core, target] + r.arrived[job][target]
             r.outward[job][target] = value.astype(r.outward[job].dtype)
             row_copy(job, target, chip).start()
 
-        repeat(1, chips, turn)
-
     def job_end(job):
-        def add(k, total):
-            source = lax.rem(chip + chips - k, chips)
-            row_copy(job, source, source).wait_recv()
-            return total + r.inward[job][source].astype(f32)
-
-        total = lax.fori_loop(1, chips, add, r.parts[job][core, chip] + r.arrived[job][chip])
+        total = r.parts[job][core, chip] + r.arrived[job][chip]
+        for k in range(1, chips):
+            row_copy(job, chip, lax.rem(chip + k, chips)).wait_recv()
+        for k in range(1, chips):
+            total += r.inward[job][lax.rem(chip + k, chips)].astype(f32)
         start = sum(JOB_ROWS[:job])
         r.packed[start : start + JOB_ROWS[job]] = total
-        repeat(1, chips, lambda k: row_copy(job, lax.rem(chip + k, chips), chip).wait_send())
+        for k in range(1, chips):
+            row_copy(job, lax.rem(chip + k, chips), chip).wait_send()
 
     def fill_head():
         part, third, fourth = r.parts[0], grads[2], grads[3]
@@ -455,7 +456,8 @@
                 part[half, i, row * 8 : row * 8 + 8] = third[at(i * 8, 8, 8), lanes]
                 part[half, i, 16 + row * 16 : 32 + row * 16] = fourth[at(i * 16, 16), lanes]
 
-        repeat(0, chips, turn)
+        for i in range(chips):
+            turn(i)
         core_copy(0).start()
 
     def fill_spatial():
@@ -472,7 +474,8 @@
                 part[half, i, 0:40] = side_by_side(top, bottom, half)
                 part[half, i, 40:48] = filler
 
-        repeat(0, chips, turn)
+        for i in range(chips):
+            turn(i)
         core_copy(1).start()
 
     def fill_sums():
@@ -488,7 +491,8 @@
             for half in range(2):
                 part[half, i] = rows
 
-        repeat(0, chips, turn)
+        for i in range(chips):
+            turn(i)
         core_copy(2).start()
 
     def fill_reduce():
@@ -501,7 +505,8 @@
             for half in range(2):
                 part[half, i] = side_by_side(gy2[at(i * 16, 8, 8)], gy2[at(i * 16 + 8, 8, 8)], half)
 
-        repeat(0, chips, turn)
+        for i in range(chips):
+            turn(i)
         core_copy(3).start()
 
     for load in query_loads(0) + key_loads:
@@ -786,17 +791,18 @@
                 here = row == images + i * slots + slot
                 owner = jnp.where(here, i, owner)
                 live = jnp.where(here, jnp.where(slot < counts[m, i], 1.0, 0.0), live)
-        embedding = e * inverse
-        key_blocks = [
+        key_rows = [
             jnp.concatenate(
                 [keys[pl.ds(m * devices * 8 + c * BLOCKS + block, devices, stride=8)] for c in range(images)], axis=0)
             for block in range(BLOCKS)
         ]
-        logits = sum(
-            dot_exact(embedding[:, block * 128 : (block + 1) * 128], key_blocks[block], ((1,), (1,)))
-            for block in range(BLOCKS)
-        )
-        logits = logits / TEMP
+        key_high, key_low = two_parts(jnp.concatenate(key_rows, axis=1))
+        logits = lax.dot_general(
+            jnp.concatenate(two_parts(e * inverse), axis=0), jnp.concatenate([key_high, key_low], axis=0),
+            (((1,), (1,)), ((), ())), preferred_element_type=f32)
+        count = devices * images
+        logits = logits[0:crops] + logits[crops:]
+        logits = (logits[:, 0:count] + logits[:, count:]) / TEMP
         top = jnp.max(logits, axis=-1, keepdims=True)
         powers = jnp.exp(logits - top)
         total = jnp.sum(powers, axis=-1, keepdims=True)
@@ -806,7 +812,9 @@
         ce = (top + jnp.log(total) - chosen) * live
         loss_sum[...] += jnp.sum(ce, axis=0, keepdims=True)
         toward = (powers / total - jnp.where(mine, 1.0, 0.0)) * (live / TEMP)
-        back = jnp.concatenate([dot_exact(toward, block, ((1,), (0,))) for block in key_blocks], axis=1)
+        back = dot(jnp.concatenate(two_parts(toward), axis=0), jnp.concatenate([key_high, key_low], axis=1))
+        back = back[0:crops] + back[crops:]
+        back = back[:, 0:COUT] + back[:, COUT:]
         de = inverse * back - e * (inverse * inverse * inverse * jnp.sum(e * back, axis=-1, keepdims=True))
         de = de * jnp.where(row < images, 1.0 / big.out_area, 1.0 / small.out_area)
         sum0 = jnp.sum(de * joined(1), axis=0, keepdims=True)

time: 137 us -> 135 us (0.985)
  Pallas kernels: 128 us -> 126 us
    pallas_call x1, Pallas kernels: 127 us -> 124 us  [step_pass(): pl.pallas_call(functools.partial(step_kernel, axes, own, slots, names), o...]
where the time goes in v3:
time: 135 us
  Pallas kernels  126 us (93%)
  local copies, waits for them, and re-layouts  7.93 us (6%)
    pallas_call x1, Pallas kernels, step_pass(): pl.pallas_call(functools.partial(step_kernel, axes, own, slots, names), o...  124 us
    unnamed x4, local copies, waits for them, and re-layouts  7.93 us

profile of v3, /device:TPU:0, one launch (start us, length us, event | category | flops | bytes accessed | tf_op | source)
XLA Modules:
  0.0 134.5 jit_solution(5852732612308288769)
XLA Ops:
  0.6 124.3 %step.1 = (bf16[2,6272,256]{2,1,0:T(8,128)(2,1)}, bf16[2,3456,256]{2,1,0:T(8,128)(2,1)}, f32[128,128]{1,0:T(8,128)}) custom-call(bf16[2,6272,256]{2,1,0:T(8,128)(2,1)} %bitcast.9, bf16[2,3456,256]{2,1,0:T(8,128)(2,1)} %bitcast.12, bf16[2,6272,256]{2,1,0:T(8,128)(2,1)} %bitcast.10, s32[2,2]{1,0:T(2,128)} %refs_3_.1, s32[2,2]{1,0:T(2,128)} %refs_4_.1, ...), custom_call_target="tpu_custom_call" | custom-call | tf_op jit(solution)/shard_map/step/pallas_call | solution.py:1083
  125.0 1.6 %finish.1 = (f32[1,1]{1,0:T(1,128)}, f32[16,64]{1,0:T(8,128)}, f32[64,72]{1,0:T(8,128)}, f32[8,256]{1,0:T(8,128)}, f32[16,256]{1,0:T(8,128)}, /*index=5*/f32[1280]{0:T(1024)}, f32[1280]{0:T(1024)}) custom-call(f32[128,128]{1,0:T(8,128)} %get-tuple-element.19.packed), custom_call_target="tpu_custom_call" | custom-call | tf_op jit(solution)/shard_map/finish/pallas_call | solution.py:1113
  126.6 0.0 copy-start
  126.6 6.1 %copy.28 = bf16[2,2,56,56,256]{4,3,2,1,0:T(8,128)(2,1)} copy(bf16[2,2,56,56,256]{4,3,2,1,0:T(8,128)(2,1)} %bitcast.11) | data formatting | bytes 12845056
  132.7 0.0 copy-done
  132.8 1.8 %copy.29 = bf16[2,2,3,24,24,256]{5,4,3,2,1,0:T(8,128)(2,1)} copy(bf16[2,2,3,24,24,256]{5,4,3,2,1,0:T(8,128)(2,1)S(1)} %bitcast.13) | data formatting | bytes 7077888
Async XLA Ops:
  126.6 6.1 %copy-start = (bf16[2,3456,256]{2,1,0:T(8,128)(2,1)S(1)}, bf16[2,3456,256]{2,1,0:T(8,128)(2,1)}, u32[]{:S(2)}) copy-start(bf16[2,3456,256]{2,1,0:T(8,128)(2,1)} %get-tuple-element.22) | copy-start | bytes 10616836

commit v4 on v3

--- a/solution.py
+++ b/solution.py
@@ -61,8 +61,9 @@
 MOMENTUM = 0.999
 MESH = pl.DeviceIdType.MESH
 PACK = 96
+QUICK = 2
 JOB_ROWS = (48, 48, 24, 8)
-TURN_ROWS = (24, 8, 16)
+TURN_ROWS = (8, 24, 16)
 
 
 def line(vector, start):
@@ -177,6 +178,17 @@
         return 0
 
     lax.fori_loop(0, chips // 2, pairs, 0)
+
+
+def unpacked_reduce(quick, chips, key_weight, query_weight):
+    for i in range(chips):
+        first, second = (quick[core, i % 4, i // 4].astype(f32) for core in range(2))
+        left = lax.broadcasted_iota(jnp.int32, (16, 128), 1) < 64
+        top = jnp.where(left, first, pltpu.roll(second, 64, 1))
+        bottom = jnp.where(left, pltpu.roll(first, 64, 1), second)
+        for k, weight in enumerate((key_weight, query_weight)):
+            rows = slice(k * 8, k * 8 + 8)
+            weight[i * 16 : (i + 1) * 16] = jnp.concatenate([top[rows], bottom[rows]], axis=0).astype(bf16)
 
 
 def stage_widths(devices):
@@ -254,14 +266,15 @@
         return place(flipped(me, flip))
 
     def gather_copies(which, stage):
+        whole = r.quick if which == QUICK else r.gathered.at[which]
         if stage == 0:
-            here = r.gathered.at[which, core, xy, z]
+            here = whole.at[core, xy, z]
             flips = [8 * k for k in range(1, chips // 4)]
         elif stage == 1:
-            here = r.gathered.at[which, core, xy]
+            here = whole.at[core, xy]
             flips = [2 * k for k in range(1, 4)]
         else:
-            here = r.gathered.at[which, core]
+            here = whole.at[core]
             flips = [1]
         return [
             remote(here, here, r.gather_send.at[which, stage, k], r.gather_recv.at[which, stage, k], partner(flip))
@@ -353,10 +366,6 @@
         start = m * first_row + c * big.area
         wide[at(start, big.area)] = dot(field[at(key_base + (2 * m + c) * big.area, big.area)], wk[0][...])
         put_moments(m, 0, c * 2, start, big.area, 112)
-        start = m * first_row + spare
-        key_side(2 * m + c, start)
-        for block in range(BLOCKS):
-            put_moments(m, 0, 8 + (c * BLOCKS + block) * 2, start + block * big.out_area, big.out_area, 112)
 
     def key_b(m, c):
         scale, bias = affine(combined(m, 0, c * 2, (1 - c) * 2, area), 0)
@@ -373,6 +382,10 @@
         for k in range(big.half):
             wide[pl.ds(start + k * big.half, big.half)] = value[k * big.wide : k * big.wide + big.half]
         put_moments(m, 1, c * 2, start, big.out_area, 112)
+        start = m * first_row + c * big.area
+        key_side(2 * m + c, start)
+        for block in range(BLOCKS):
+            put_moments(m, 1, 8 + (c * BLOCKS + block) * 2, start + block * big.out_area, big.out_area, 112)
 
     def key_c(m, c):
         scale, bias = affine(combined(m, 1, c * 2, (1 - c) * 2, out_area), CMID)
@@ -393,7 +406,7 @@
             lanes = 2 * CMID + block * 128
             row, other = (c * BLOCKS + block) * 2, ((1 - c) * BLOCKS + block) * 2
             scale3, bias3 = affine(combined(m, 2, row, other, out_area), lanes)
-            scale4, bias4 = affine(combined(m, 0, 8 + row, 8 + other, out_area), lanes + COUT)
+            scale4, bias4 = affine(combined(m, 1, 8 + row, 8 + other, out_area), lanes + COUT)
             bias = bias3 + bias4
             e = jnp.zeros((8, 128), f32)
             for k in range(big.out_area // 112):
@@ -521,20 +534,21 @@
         packed_shards(current, r.sent, 1)
         for which in range(2):
             r.gathered[which, core, xy, z] = r.sent[which]
+        r.quick[core, xy, z] = jnp.concatenate([r.sent[k, 0:16].astype(f32)[0:8] for k in range(2)], axis=0).astype(bf16)
     else:
         for shard, w in zip((r.r0, r.s0, r.e0, r.p0, r.r1, r.s1, r.e1, r.p1), wq + wk):
             w[...] = shard[...]
     if devices > 1:
         pl.semaphore_wait(barrier, devices - 1)
     if own:
-        gather_start(0, 0)
+        gather_start(QUICK, 0)
     for ref in list(planes_of.values()) + list(back_of.values()) + list(stage_of.values()) + grads + [
         r.raised, gain_sum, shift_sum, loss_sum, gy2] + [pair[0] for pair in moved]:
         ref[...] = jnp.zeros_like(ref)
     if own:
-        gather_end(0, 0)
-        gather_start(0, 1)
-        gather_start(1, 0)
+        gather_end(QUICK, 0)
+        gather_start(QUICK, 1)
+        gather_start(0, 0)
 
     def micro_step(m):
         opening, closing = m == 0, m == micros - 1
@@ -598,25 +612,31 @@
 
         @pl.when(opening)
         def _():
+            if own:
+                gather_end(QUICK, 1)
+                gather_start(QUICK, 2)
+                gather_end(0, 0)
+                gather_start(0, 1)
+                gather_start(1, 0)
             for load in key_loads:
                 load.wait()
             repeat(0, 2 * micros, key_even)
+            if own:
+                gather_end(QUICK, 2)
+                unpacked_reduce(r.quick, chips, wk[0], wq[0])
+            repeat(0, 2, lambda c: key_a(0, c))
+            exchange_start(0, 0)
             if own:
                 gather_end(0, 1)
                 gather_start(0, 2)
                 gather_end(1, 0)
                 gather_start(1, 1)
-                gather_end(0, 2)
-                unpacked(r.gathered, 0, chips, wk, gy2)
-            repeat(0, 2, lambda c: key_a(0, c))
-            exchange_start(0, 0)
-            if own:
-                gather_end(1, 1)
-                gather_start(1, 2)
             repeat(0, 2, lambda c: key_a(1, c))
             exchange_start(1, 0)
             for load in query_loads(1):
                 load.start()
+
+        def prepare_weights():
             if own:
                 gather_end(1, 2)
                 unpacked(r.gathered, 1, chips, wq, gy2)
@@ -657,10 +677,16 @@
 
         @pl.when(opening)
         def _():
+            if own:
+                gather_end(0, 2)
+                unpacked(r.gathered, 0, chips, wk, gy2)
+                gather_end(1, 1)
+                gather_start(1, 2)
             for k in range(2):
                 exchange_end(k, 0)
                 repeat(0, 2, lambda c: key_b(k, c))
                 exchange_start(k, 1)
+            prepare_weights()
 
         sums[...] = jnp.zeros_like(sums)
 
@@ -1072,11 +1098,11 @@
     if own:
         scratch |= {n: buf(f32, *shape) for n, shape in totals.items()}
         scratch |= dict(
-            sent=buf(bf16, 2, PACK, 128), gathered=buf(bf16, 2, 2, 4, 4, PACK, 128),
+            sent=buf(bf16, 2, PACK, 128), gathered=buf(bf16, 2, 2, 4, 4, PACK, 128), quick=buf(bf16, 2, 4, 4, 16, 128),
             parts=[buf(f32, 2, chips, n, 128) for n in JOB_ROWS], arrived=[buf(f32, chips, n, 128) for n in JOB_ROWS],
             outward=[buf(t, chips, n, 128) for n, t in zip(JOB_ROWS, wires)],
             inward=[buf(t, chips, n, 128) for n, t in zip(JOB_ROWS, wires)],
-            gather_send=dma(2, 3, 3), gather_recv=dma(2, 3, 3), core_send=dma(4), core_recv=dma(4),
+            gather_send=dma(3, 3, 3), gather_recv=dma(3, 3, 3), core_send=dma(4), core_recv=dma(4),
             row_send=dma(4, chips), row_recv=dma(4, chips),
         )
     names = list(inputs) + list(outputs) + list(scratch)

time: 135 us -> 136 us (level)
  no operation moved by 1% of the time
where the time goes in v4:
time: 136 us
  Pallas kernels  127 us (93%)
  local copies, waits for them, and re-layouts  7.93 us (6%)
    pallas_call x1, Pallas kernels, step_pass(): pl.pallas_call(functools.partial(step_kernel, axes, own, slots, names), o...  126 us
    unnamed x4, local copies, waits for them, and re-layouts  7.93 us

profile of v4, /device:TPU:0, one launch (start us, length us, event | category | flops | bytes accessed | tf_op | source)
XLA Modules:
  0.0 135.9 jit_solution(12643962778811472321)
XLA Ops:
  0.6 125.7 %step.1 = (bf16[2,6272,256]{2,1,0:T(8,128)(2,1)}, bf16[2,3456,256]{2,1,0:T(8,128)(2,1)}, f32[128,128]{1,0:T(8,128)}) custom-call(bf16[2,6272,256]{2,1,0:T(8,128)(2,1)} %bitcast.9, bf16[2,3456,256]{2,1,0:T(8,128)(2,1)} %bitcast.12, bf16[2,6272,256]{2,1,0:T(8,128)(2,1)} %bitcast.10, s32[2,2]{1,0:T(2,128)} %refs_3_.1, s32[2,2]{1,0:T(2,128)} %refs_4_.1, ...), custom_call_target="tpu_custom_call" | custom-call | tf_op jit(solution)/shard_map/step/pallas_call | solution.py:1109
  126.3 1.6 %finish.1 = (f32[1,1]{1,0:T(1,128)}, f32[16,64]{1,0:T(8,128)}, f32[64,72]{1,0:T(8,128)}, f32[8,256]{1,0:T(8,128)}, f32[16,256]{1,0:T(8,128)}, /*index=5*/f32[1280]{0:T(1024)}, f32[1280]{0:T(1024)}) custom-call(f32[128,128]{1,0:T(8,128)} %get-tuple-element.19.packed), custom_call_target="tpu_custom_call" | custom-call | tf_op jit(solution)/shard_map/finish/pallas_call | solution.py:1139
  128.0 0.0 copy-start
  128.0 6.1 %copy.28 = bf16[2,2,56,56,256]{4,3,2,1,0:T(8,128)(2,1)} copy(bf16[2,2,56,56,256]{4,3,2,1,0:T(8,128)(2,1)} %bitcast.11) | data formatting | bytes 12845056
  134.1 0.0 copy-done
  134.1 1.8 %copy.29 = bf16[2,2,3,24,24,256]{5,4,3,2,1,0:T(8,128)(2,1)} copy(bf16[2,2,3,24,24,256]{5,4,3,2,1,0:T(8,128)(2,1)S(1)} %bitcast.13) | data formatting | bytes 7077888
Async XLA Ops:
  128.0 6.1 %copy-start = (bf16[2,3456,256]{2,1,0:T(8,128)(2,1)S(1)}, bf16[2,3456,256]{2,1,0:T(8,128)(2,1)}, u32[]{:S(2)}) copy-start(bf16[2,3456,256]{2,1,0:T(8,128)(2,1)} %get-tuple-element.22) | copy-start | bytes 10616836

commit v5 on v3

--- a/solution.py
+++ b/solution.py
@@ -240,15 +240,21 @@
                 r.query_load.at[m, 1]),
         ]
 
-    def store_big(m, c):
-        return pltpu.make_async_copy(
-            field.at[pl.ds(m * field_rows + c * big.area, big.area)],
-            r.big_out.at[m, pl.ds(c * big.area, big.area)], r.store.at[m, c])
-
-    def store_small(m):
-        return pltpu.make_async_copy(
-            field.at[pl.ds(m * field_rows + small.row, field_rows - small.row)], r.small_out.at[m],
-            r.store.at[m, images])
+    def field_stores(m):
+        return [
+            pltpu.make_async_copy(slope1.at[pl.ds(0, small.row)], r.da_big.at[m], r.store.at[m, 0]),
+            pltpu.make_async_copy(slope1.at[pl.ds(small.row, field_rows - small.row)], r.da_small.at[m], r.store.at[m, 1]),
+        ]
+
+    def even_stores(m):
+        return [
+            pltpu.make_async_copy(even.at[pl.ds(0, small.out_row)], r.even_big.at[m], r.store.at[m, 2]),
+            pltpu.make_async_copy(even.at[pl.ds(small.out_row, outs - small.out_row)], r.even_small.at[m], r.store.at[m, 3]),
+        ]
+
+    def settle(copies):
+        for copy in copies:
+            copy.wait()
 
     def partner(flip):
         return place(flipped(me, flip))
@@ -529,7 +535,7 @@
     if own:
         gather_start(0, 0)
     for ref in list(planes_of.values()) + list(back_of.values()) + list(stage_of.values()) + grads + [
-        r.raised, gain_sum, shift_sum, loss_sum, gy2] + [pair[0] for pair in moved]:
+        gain_sum, shift_sum, loss_sum, gy2] + [pair[0] for pair in moved]:
         ref[...] = jnp.zeros_like(ref)
     if own:
         gather_end(0, 0)
@@ -540,7 +546,7 @@
         opening, closing = m == 0, m == micros - 1
         base = m * field_rows
         w1, w2, w3, w4 = wq
-        w1t, w3t, w4t, wt0, wt1 = (r.w1t, r.w3t, r.w4t, r.wt0, r.wt1)
+        w3t, w4t, wt0, wt1 = (r.w3t, r.w4t, r.wt0, r.wt1)
         alive_count = sum(counts[m, i] for i in range(images)).astype(f32)
         count1 = images * big.area + small.area * alive_count
         count2 = images * big.out_area + small.out_area * alive_count
@@ -592,6 +598,10 @@
                     even[at(start, kind.out_area), block * 128 : (block + 1) * 128] = value
 
                 even_cells(field, base + kind.row + (first + c) * kind.area, kind, wide_stage, dense_stage, put)
+
+        @pl.when(m > 0)
+        def _():
+            settle(even_stores(m - 1))
 
         over_big(even_batch)
         over_small(even_batch)
@@ -620,7 +630,6 @@
             if own:
                 gather_end(1, 2)
                 unpacked(r.gathered, 1, chips, wq, gy2)
-            w1t[...] = w1[...].T
             w3t[...] = w3[...].T
             w4t[...] = w4[...].T
             wt0[...] = jnp.zeros_like(wt0)
@@ -663,6 +672,10 @@
                 exchange_start(k, 1)
 
         sums[...] = jnp.zeros_like(sums)
+
+        @pl.when(m > 0)
+        def _():
+            settle(field_stores(m - 1))
 
         def hidden_batch(kind, first, count):
             scale, bias = vec[3:4], vec[4:5]
@@ -856,10 +869,9 @@
             grad3, gradp = d3[0:size], dp[0:size]
             gy2[at(start, size)] = dot(grad3, w3t[...])
             gradient = dot(gradp, w4t[...])
-            for block in range(2):
-                wide[at(AP + block * outs + start, size)] = gradient[:, block * 128 : (block + 1) * 128]
             grads[2][...] += dot_rows(thin[at(H2 + start, size)], grad3)
             grads[3][...] += dot_rows(even[at(start, size)], gradp)
+            even[at(start, size)] = gradient.astype(bf16)
             mean = vec[5:6]
             level, reach = jnp.zeros((8, 128), f32), jnp.zeros((8, 128), f32)
             for k in range(size // step):
@@ -873,6 +885,8 @@
 
         over_big(head_back)
         over_small(head_back)
+        for copy in even_stores(m):
+            copy.start()
 
         if own:
 
@@ -968,46 +982,18 @@
         over_big(reduce_back, *job_hooks((1,), (2,)))
         over_small(reduce_back)
 
-        if own:
-
-            @pl.when(closing)
-            def _():
-                fill_reduce()
-                job_end(0)
-
-        raised = r.raised
-
-        def field_back(kind, first, count):
-            half, side = kind.half, kind.side
-            size = count * kind.area
-            start = kind.row + first * kind.area
-            whole = dot(slope1[at(start, size)], w1t[...])
-            out_start = kind.out_row + first * kind.out_area
-            for k in range(count * half):
-                row = k * 2 * side
-                for block in range(2):
-                    lanes = slice(block * 128, (block + 1) * 128)
-                    slot = k % 4 * 2 + block
-                    raised[slot, pl.ds(0, half, stride=2)] = wide[pl.ds(AP + block * outs + out_start + k * half, half)]
-                    top_row = whole[row : row + side, lanes] + raised[slot, 0:side]
-                    both = jnp.concatenate([top_row, whole[row + side : row + 2 * side, lanes]], axis=0)
-                    field[at(base + start + row, 2 * side), lanes] = both.astype(bf16)
-            if kind is big:
-                store_big(m, first).start()
-            else:
-                store_small(m).start()
-
-        over_big(field_back, *job_hooks((), (3,)))
-        over_small(field_back)
+        for copy in field_stores(m):
+            copy.start()
 
     repeat(0, micros, micro_step)
     if own:
+        fill_reduce()
+        job_end(0)
+        job_send(3)
         for job in range(1, 4):
             job_end(job)
-    for m in range(micros):
-        for c in range(images):
-            store_big(m, c).wait()
-        store_small(m).wait()
+    settle(even_stores(micros - 1))
+    settle(field_stores(micros - 1))
 
 
 def step_pass(axes, own, slots, big, small, key, counts, mask, current, lagged, vectors):
@@ -1033,7 +1019,11 @@
         big_hbm=(big, hbm), small_hbm=(small, hbm), key_hbm=(key, hbm), counts=(counts, smem), mask=(mask, smem),
         r0=r0, s0=s0, e0=e0, p0=p0, r1=r1, s1=s1, e1=e1, p1=p1, gains=gains, shifts=shifts, gains1=gains1, shifts1=shifts1)
     outputs = dict(
-        big_out=(jax.ShapeDtypeStruct(big.shape, bf16), hbm), small_out=(jax.ShapeDtypeStruct(small.shape, bf16), hbm))
+        da_big=(jax.ShapeDtypeStruct((micros, two.row, CMID), bf16), hbm),
+        da_small=(jax.ShapeDtypeStruct((micros, rows - two.row, CMID), bf16), hbm),
+        even_big=(jax.ShapeDtypeStruct((micros, two.out_row, CIN), bf16), hbm),
+        even_small=(jax.ShapeDtypeStruct((micros, outs - two.out_row, CIN), bf16), hbm),
+        w1q=(jax.ShapeDtypeStruct((CIN, CMID), bf16), vmem))
     if own:
         outputs |= dict(packed=(jax.ShapeDtypeStruct((sum(JOB_ROWS), 128), f32), vmem))
     else:
@@ -1055,19 +1045,19 @@
         back_big=buf(bf16, one.count, one.half + 1, one.wide, 256),
         back_small=buf(bf16, two.count, two.half + 1, two.wide, 256),
         gy2=buf(f32, outs + 16, 128), stage_big=buf(f32, 2, 2, 80, 128), stage_small=buf(f32, 2, 2, 48, 128),
-        wide_stage=buf(f32, 8, SIDE, 128), dense_stage=buf(f32, 2, one.out_area, 128), raised=buf(f32, 8, SIDE, 128),
+        wide_stage=buf(f32, 8, SIDE, 128), dense_stage=buf(f32, 2, one.out_area, 128),
         d3=buf(bf16, two.count * two.out_area, COUT), dp=buf(bf16, two.count * two.out_area, COUT),
-        w1t=buf(bf16, CMID, CIN), w3t=buf(bf16, COUT, CMID), w4t=buf(bf16, COUT, CIN),
+        w3t=buf(bf16, COUT, CMID), w4t=buf(bf16, COUT, CIN),
         wt0=buf(bf16, 256, 256), wt1=buf(bf16, 512, 256), sums=buf(f32, 18, 8, 128), vec=buf(f32, 80, 128),
         rows_e=buf(f32, 4, BLOCKS, crops, 128), rows_c=buf(f32, 2, BLOCKS, crops, 128),
         keys=buf(f32, devices * 16, 128), embed=buf(f32, 16, 128),
         moved=[[buf(f32, 1 << width, n, 128) for width in widths] for _ in range(micros) for n in TURN_ROWS],
-        key_load=dma(2 * micros), query_load=dma(micros, 2), store=dma(micros, images + 1),
+        key_load=dma(2 * micros), query_load=dma(micros, 2), store=dma(micros, 4),
         move_send=dma(3 * micros, 2, 1 << widths[0]), move_recv=dma(3 * micros, 2, 1 << widths[0]),
         key_send=dma(micros, devices), key_recv=dma(micros, devices),
     )
     first, second, third, fourth = (buf(bf16, *shape) for shape in weights)
-    scratch |= dict(w1q=first, w2q=second, w3q=third, w4q=fourth, w1k=first, w2k=second, w3k=third, w4k=fourth)
+    scratch |= dict(w2q=second, w3q=third, w4q=fourth, w1k=first, w2k=second, w3k=third, w4k=fourth)
     wires = (bf16, bf16, f32, f32)
     if own:
         scratch |= {n: buf(f32, *shape) for n, shape in totals.items()}
@@ -1092,7 +1082,7 @@
     return types.SimpleNamespace(**dict(zip(outputs, out)))
 
 
-def finish_kernel(packed, loss, reduce_out, spatial_out, expand_out, shortcut_out, gains, shifts):
+def write_sums(packed, loss, reduce_out, spatial_out, expand_out, shortcut_out, gains, shifts):
     reduce_out[0:8] = packed[120:128, 0:64]
     reduce_out[8:16] = packed[120:128, 64:128]
     rows = jnp.concatenate([packed[48:88], jnp.zeros((88, 128), f32)], axis=0).T
@@ -1107,16 +1097,72 @@
     loss[...] = packed[106:107, 0:1]
 
 
-def finish_pass(packed):
-    vmem = pl.BlockSpec(memory_space=pltpu.VMEM)
-    shapes = [(1, 1), (16, 64), (64, 72), (8, 256), (16, 256), (NORMS,), (NORMS,)]
+def field_kernel(own, fields, da_big, da_small, even_big, even_small, weight, *refs):
+    big, small = fields
+    packed, refs = (refs[0], refs[1:]) if own else (None, refs)
+    big_out, small_out = refs[:2]
+    raised, cells = refs[-2:]
+    part = pl.program_id(1)
+
+    @pl.when(jnp.logical_and(pl.program_id(0) == 0, part == 0))
+    def _():
+        raised[...] = jnp.zeros_like(raised)
+        if own:
+            write_sums(packed, *refs[2:-2])
+
+    def gradient(kind, count, da, shortcut, out):
+        half, side = kind.half, kind.side
+        whole = lax.dot_general(da[...], weight[...], (((1,), (1,)), ((), ())), preferred_element_type=f32)
+        for block in range(2):
+            lanes = slice(block * 128, (block + 1) * 128)
+            cells[block, 0 : count * kind.out_area] = shortcut[:, lanes].astype(f32)
+        for k in range(count * half):
+            row = k * 2 * side
+            for block in range(2):
+                lanes = slice(block * 128, (block + 1) * 128)
+                slot = k % 4 * 2 + block
+                raised[slot, pl.ds(0, half, stride=2)] = cells[block, k * half : (k + 1) * half]
+                upper = whole[row : row + side, lanes] + raised[slot, 0:side]
+                both = jnp.concatenate([upper, whole[row + side : row + 2 * side, lanes]], axis=0)
+                out[row : row + 2 * side, lanes] = both.astype(bf16)
+
+    @pl.when(part < big.count)
+    def _():
+        gradient(big, 1, da_big, even_big, big_out)
+
+    @pl.when(part >= big.count)
+    def _():
+        gradient(small, small.count // 2, da_small, even_small, small_out)
+
+
+def field_pass(own, slots, images, step):
+    micros = step.da_big.shape[0]
+    fields = field_pair(images, slots)
+    big, small = fields
+    pair = small.count // 2
+    whole = pl.BlockSpec(memory_space=pltpu.VMEM)
+
+    def large(rows, lanes):
+        return pl.BlockSpec((None, rows, lanes), lambda m, j: (m, jnp.minimum(j, big.count - 1), 0))
+
+    def little(rows, lanes):
+        return pl.BlockSpec((None, rows, lanes), lambda m, j: (m, jnp.maximum(j - big.count, 0), 0))
+
+    outs = [jax.ShapeDtypeStruct((micros, big.count * big.area, CIN), bf16), jax.ShapeDtypeStruct((micros, small.count * small.area, CIN), bf16)]
+    sums = [(1, 1), (16, 64), (64, 72), (8, 256), (16, 256), (NORMS,), (NORMS,)] if own else []
     return pl.pallas_call(
-        finish_kernel,
-        out_shape=[jax.ShapeDtypeStruct(shape, f32) for shape in shapes],
-        in_specs=[vmem],
-        out_specs=[vmem] * 7,
-        name="finish",
-    )(packed)
+        functools.partial(field_kernel, own, fields),
+        grid=(micros, big.count + 2),
+        out_shape=outs + [jax.ShapeDtypeStruct(shape, f32) for shape in sums],
+        in_specs=[
+            large(big.area, CMID), little(pair * small.area, CMID), large(big.out_area, CIN),
+            little(pair * small.out_area, CIN), whole,
+        ] + [whole] * own,
+        out_specs=[large(big.area, CIN), little(pair * small.area, CIN)] + [whole] * len(sums),
+        scratch_shapes=[pltpu.VMEM((8, SIDE, 128), f32), pltpu.VMEM((2, pair * small.out_area if pair * small.out_area > big.out_area else big.out_area, 128), f32)],
+        compiler_params=pltpu.CompilerParams(vmem_limit_bytes=58 * 2**20, dimension_semantics=("arbitrary", "arbitrary")),
+        name="field",
+    )(step.da_big, step.da_small, step.even_big, step.even_small, step.w1q, *([step.packed] if own else []))
 
 
 def gather_weights(shards):
@@ -1143,9 +1189,10 @@
         axes, own, slots, query_global.reshape(micros, -1, CIN), small_crop_query.reshape(micros, -1, CIN),
         key_global.reshape(micros, -1, CIN), small_count, shuffle_mask, current, lagged, vectors,
     )
-    fields = (out.big_out.reshape(query_global.shape), out.small_out.reshape(small_crop_query.shape))
+    big_out, small_out, *sums = field_pass(own, slots, query_global.shape[1], out)
+    fields = (big_out.reshape(query_global.shape), small_out.reshape(small_crop_query.shape))
     if own:
-        loss, first, second, third, fourth, gains_grad, shifts_grad = finish_pass(out.packed)
+        loss, first, second, third, fourth, gains_grad, shifts_grad = sums
         return (loss.reshape(()), *fields, first, second.T, third, fourth, gains_grad, shifts_grad)
     totals = (out.g1.T, out.g2.T, out.g3, out.g4)
     summed = lax.psum_scatter(totals, "dp", scatter_dimension=0, tiled=True)

time: 135 us -> 134 us (level)
  local copies, waits for them, and re-layouts: 7.93 us -> 0 us
  Pallas kernels: 126 us -> 133 us
    pallas_call x1, Pallas kernels: 1.63 us -> 11 us  [field_pass(): pl.pallas_call(functools.partial(field_kernel, own, fields), grid=(micros...]
    unnamed x4 -> x0, local copies, waits for them, and re-layouts: 7.93 us -> none
    pallas_call x1, Pallas kernels: 124 us -> 122 us  [step_pass(): pl.pallas_call(functools.partial(step_kernel, axes, own, slots, names), o...]
where the time goes in v5:
time: 134 us
  Pallas kernels  133 us (99%)
    pallas_call x1, Pallas kernels, step_pass(): pl.pallas_call(functools.partial(step_kernel, axes, own, slots, names), o...  122 us
    pallas_call x1, Pallas kernels, field_pass(): pl.pallas_call(functools.partial(field_kernel, own, fields), grid=(micros...  11 us

profile of v5, /device:TPU:0, one launch (start us, length us, event | category | flops | bytes accessed | tf_op | source)
XLA Modules:
  0.0 134.1 jit_solution(7215729939983583829)
XLA Ops:
  0.6 122.3 %step.1 = (bf16[2,6272,128]{2,1,0:T(8,128)(2,1)}, bf16[2,3456,128]{2,1,0:T(8,128)(2,1)}, bf16[2,1568,256]{2,1,0:T(8,128)(2,1)}, bf16[2,864,256]{2,1,0:T(8,128)(2...) custom-call(bf16[2,6272,256]{2,1,0:T(8,128)(2,1)} %bitcast.9, bf16[2,3456,256]{2,1,0:T(8,128)(2,1)} %bitcast.11, ...), custom_call_target="tpu_custom_call" | custom-call | tf_op jit(solution)/shard_map/step/pallas_call | solution.py:1073
  123.0 11.0 %field.1 = (bf16[2,6272,256]{2,1,0:T(8,128)(2,1)}, bf16[2,3456,256]{2,1,0:T(8,128)(2,1)}, f32[1,1]{1,0:T(1,128)}, f32[16,64]{1,0:T(8,128)}, f32[64,72]{1,0:T(8,1...) custom-call(bf16[2,6272,128]{2,1,0:T(8,128)(2,1)} %get-tuple-element.24.da_big, ...), custom_call_target="tpu_custom_call" | custom-call | tf_op jit(solution)/shard_map/field/pallas_call | solution.py:1153

commit v6 on v5

--- a/solution.py
+++ b/solution.py
@@ -630,6 +630,7 @@
             if own:
                 gather_end(1, 2)
                 unpacked(r.gathered, 1, chips, wq, gy2)
+            r.w1t[...] = w1[...].T
             w3t[...] = w3[...].T
             w4t[...] = w4[...].T
             wt0[...] = jnp.zeros_like(wt0)
@@ -1023,7 +1024,7 @@
         da_small=(jax.ShapeDtypeStruct((micros, rows - two.row, CMID), bf16), hbm),
         even_big=(jax.ShapeDtypeStruct((micros, two.out_row, CIN), bf16), hbm),
         even_small=(jax.ShapeDtypeStruct((micros, outs - two.out_row, CIN), bf16), hbm),
-        w1q=(jax.ShapeDtypeStruct((CIN, CMID), bf16), vmem))
+        w1t=(jax.ShapeDtypeStruct((CMID, CIN), bf16), vmem))
     if own:
         outputs |= dict(packed=(jax.ShapeDtypeStruct((sum(JOB_ROWS), 128), f32), vmem))
     else:
@@ -1057,7 +1058,7 @@
         key_send=dma(micros, devices), key_recv=dma(micros, devices),
     )
     first, second, third, fourth = (buf(bf16, *shape) for shape in weights)
-    scratch |= dict(w2q=second, w3q=third, w4q=fourth, w1k=first, w2k=second, w3k=third, w4k=fourth)
+    scratch |= dict(w1q=first, w2q=second, w3q=third, w4q=fourth, w1k=first, w2k=second, w3k=third, w4k=fourth)
     wires = (bf16, bf16, f32, f32)
     if own:
         scratch |= {n: buf(f32, *shape) for n, shape in totals.items()}
@@ -1112,19 +1113,21 @@
 
     def gradient(kind, count, da, shortcut, out):
         half, side = kind.half, kind.side
-        whole = lax.dot_general(da[...], weight[...], (((1,), (1,)), ((), ())), preferred_element_type=f32)
         for block in range(2):
             lanes = slice(block * 128, (block + 1) * 128)
             cells[block, 0 : count * kind.out_area] = shortcut[:, lanes].astype(f32)
-        for k in range(count * half):
-            row = k * 2 * side
-            for block in range(2):
-                lanes = slice(block * 128, (block + 1) * 128)
-                slot = k % 4 * 2 + block
-                raised[slot, pl.ds(0, half, stride=2)] = cells[block, k * half : (k + 1) * half]
-                upper = whole[row : row + side, lanes] + raised[slot, 0:side]
-                both = jnp.concatenate([upper, whole[row + side : row + 2 * side, lanes]], axis=0)
-                out[row : row + 2 * side, lanes] = both.astype(bf16)
+        pairs = 1 if kind is big else 3
+        for first in range(0, count * half, pairs):
+            whole = dot(da[first * 2 * side : (first + pairs) * 2 * side], weight[...])
+            for k in range(pairs):
+                row, line_of = k * 2 * side, first + k
+                for block in range(2):
+                    lanes = slice(block * 128, (block + 1) * 128)
+                    slot = line_of % 4 * 2 + block
+                    raised[slot, pl.ds(0, half, stride=2)] = cells[block, line_of * half : (line_of + 1) * half]
+                    upper = whole[row : row + side, lanes] + raised[slot, 0:side]
+                    both = jnp.concatenate([upper, whole[row + side : row + 2 * side, lanes]], axis=0)
+                    out[line_of * 2 * side : (line_of + 1) * 2 * side, lanes] = both.astype(bf16)
 
     @pl.when(part < big.count)
     def _():
@@ -1162,7 +1165,7 @@
         scratch_shapes=[pltpu.VMEM((8, SIDE, 128), f32), pltpu.VMEM((2, pair * small.out_area if pair * small.out_area > big.out_area else big.out_area, 128), f32)],
         compiler_params=pltpu.CompilerParams(vmem_limit_bytes=58 * 2**20, dimension_semantics=("arbitrary", "arbitrary")),
         name="field",
-    )(step.da_big, step.da_small, step.even_big, step.even_small, step.w1q, *([step.packed] if own else []))
+    )(step.da_big, step.da_small, step.even_big, step.even_small, step.w1t, *([step.packed] if own else []))
 
 
 def gather_weights(shards):

time: 134 us -> 134 us (level)
  no operation moved by 1% of the time
where the time goes in v6:
time: 134 us
  Pallas kernels  133 us (99%)
    pallas_call x1, Pallas kernels, step_pass(): pl.pallas_call(functools.partial(step_kernel, axes, own, slots, names), o...  122 us
    pallas_call x1, Pallas kernels, field_pass(): pl.pallas_call(functools.partial(field_kernel, own, fields), grid=(micros...  10.9 us

profile of v6, /device:TPU:0, one launch (start us, length us, event | category | flops | bytes accessed | tf_op | source)
XLA Modules:
  0.0 134.0 jit_solution(4387141182520525300)
XLA Ops:
  0.6 122.3 %step.1 = (bf16[2,6272,128]{2,1,0:T(8,128)(2,1)}, bf16[2,3456,128]{2,1,0:T(8,128)(2,1)}, bf16[2,1568,256]{2,1,0:T(8,128)(2,1)}, bf16[2,864,256]{2,1,0:T(8,128)(2...) custom-call(bf16[2,6272,256]{2,1,0:T(8,128)(2,1)} %bitcast.9, bf16[2,3456,256]{2,1,0:T(8,128)(2,1)} %bitcast.11, ...), custom_call_target="tpu_custom_call" | custom-call | tf_op jit(solution)/shard_map/step/pallas_call | solution.py:1074
  123.0 10.9 %field.1 = (bf16[2,6272,256]{2,1,0:T(8,128)(2,1)}, bf16[2,3456,256]{2,1,0:T(8,128)(2,1)}, f32[1,1]{1,0:T(1,128)}, f32[16,64]{1,0:T(8,128)}, f32[64,72]{1,0:T(8,1...) custom-call(bf16[2,6272,128]{2,1,0:T(8,128)(2,1)} %get-tuple-element.24.da_big, ...), custom_call_target="tpu_custom_call" | custom-call | tf_op jit(solution)/shard_map/field/pallas_call | solution.py:1156
